TPU v7x, 32 devices: a whole 2x2x4 slice. The times are simulated.
32 devices in a mesh: row: 8 (over y, x, core), col: 4 (over z).
Axes of the slice: x: 2, y: 2, z: 4, core: 2. Of those that a mesh axis runs over, the one named last changes fastest.
Arguments:
- source_points: bfloat16 [32768, 1024], P('row'), may hold values from -8 to 8
- target_points: bfloat16 [16384, 1024], P('col', 'row'), may hold values from -8 to 8
- source_mass: float32 [32768], P('row'), may hold values from 0.25 to 4
- target_mass: float32 [16384], P('col'), may hold values from 0.25 to 4
- tile_index: int32 [128, 8], P('row', 'col'), may hold values from 0 to 15, as said below
- tile_count: int32 [128, 4], P('row', 'col'), may hold values from 1 to 2, as said below
Outputs:
- source_potential: float32 [32768], P('row')
- target_potential: float32 [16384], P('col')
Inputs may be any that keep to these rules, and one draw needn't show every extreme that they name: `tile_index`: within the 2 slots of one source tile and one index of col the target tiles are distinct; every target tile is named by a live slot of some source tile. `tile_count`: each index of row holds, for every index of col, a source tile with all 2 slots live.
All inputs are finite; a program needn't handle non-finite values.
Results may differ from a plain program's by a relative error of at most 0.0003.
Values may be sent and summed in bfloat16 or wider, within the bound.
No kernel may reach another device: no remote copies, remote signals or barrier semaphores. Data moves between devices by JAX's collectives and lax.ppermute only.
A program may use at most 128 MiB of HBM per device.

v0:
```python
import math

import jax
import jax.numpy as jnp
from jax import lax
from jax.sharding import PartitionSpec as P

TILE = 256
ITERS = 3


masked_score = -1e30


def cost_terms(piece, source_points, tile_index):
    width = piece.shape[1]
    source_tiles = source_points.reshape(-1, TILE, width)
    target_tiles = piece.reshape(-1, TILE, width)
    chosen = target_tiles[tile_index]
    return jnp.einsum("rad,rkbd->rkab", source_tiles, chosen, preferred_element_type=jnp.float32)


def on_device(source_points, target_points, source_mass, target_mass, tile_index, tile_count):
    tiles_per_row = source_points.shape[0] // TILE
    col_tiles = target_points.shape[0] // TILE
    slot_count = tile_index.shape[1]
    scale = 1.0 / math.sqrt(source_points.shape[1])
    live = jnp.arange(slot_count)[None, :] < tile_count
    onehot = (tile_index[:, :, None] == jnp.arange(col_tiles)[None, None, :]) & live[:, :, None]
    log_source = jnp.log(source_mass).reshape(tiles_per_row, TILE)
    log_target = jnp.log(target_mass).reshape(col_tiles, TILE)
    target_pot = jnp.zeros((col_tiles, TILE), jnp.float32)
    source_pot = jnp.zeros((tiles_per_row, TILE), jnp.float32)
    for iteration in range(ITERS):
        cost = (
            cost_terms(
                lax.all_gather(target_points, "row", axis=1, tiled=True), source_points, tile_index
            )
            * scale
        )
        scores = cost + target_pot[tile_index][:, :, None, :]
        scores = jnp.where(live[:, :, None, None], scores, masked_score)
        row_top = jnp.max(scores, axis=(1, 3))
        highest = lax.pmax(row_top, "col")
        local_sum = jnp.sum(jnp.exp(scores - highest[:, None, :, None]), axis=(1, 3))
        total = lax.psum(local_sum, "col")
        source_pot = log_source - highest - jnp.log(total)
        columns = cost + source_pot[:, None, :, None]
        columns = jnp.where(live[:, :, None, None], columns, masked_score)
        slot_top = jnp.max(columns, axis=2)
        local_top = jnp.max(
            jnp.where(onehot[..., None], slot_top[:, :, None, :], masked_score), axis=(0, 1)
        )
        col_high = lax.pmax(local_top, "row")
        slot_ref = col_high[tile_index]
        sums = jnp.sum(jnp.exp(columns - slot_ref[:, :, None, :]), axis=2)
        col_sum = jnp.sum(jnp.where(onehot[..., None], sums[:, :, None, :], 0.0), axis=(0, 1))
        col_total = lax.psum(col_sum, "row")
        target_pot = log_target - col_high - jnp.log(col_total)
    return (source_pot.reshape(-1), target_pot.reshape(-1))


def solution(mesh):
    placed = (P("row", None), P("col", "row"), P("row"), P("col"), P("row", "col"), P("row", "col"))
    return jax.shard_map(
        on_device, mesh=mesh, in_specs=placed, out_specs=(P("row"), P("col")), check_vma=False
    )
```

profile of v0, /device:TPU:0, one launch (start us, length us, event | category | flops | bytes accessed | tf_op | source)
XLA Modules:
  0.0 388.9 jit_solution(11266303442523186377)
XLA Ops:
  7.2 0.7 all-gather.2.cloned.1.call-update
  7.9 0.8 copy.13
  8.7 0.7 compare_select_fusion
  10.2 0.7 log.24
  10.9 0.7 log.25
  11.6 0.7 iota_compare_fusion
  12.5 56.1 %all-gather.2.cloned.1.call-done = bf16[4096,1024]{1,0:T(8,128)(2,1)} async-done(((bf16[4096,128]{1,0:T(8,128)(2,1)}), bf16[4096,1024]{1,0:T(8,128)(2,1)}) %all-gather.2.cloned.1.call-update) | async-done | bytes 8388624 | tf_op jit(solution)/shard_map/all_gather | solution.py:37
  68.6 10.6 %gather_fusion = bf16[32,256,1024]{2,1,0:T(8,128)(2,1)} fusion(bf16[16,256,1024]{2,1,0:T(8,128)(2,1)} %bitcast.57, s32[1024]{0:T(1024)S(1)} %pad_clamp_fusion), kind=kCustom, calls=%fused_computation | custom fusion | bytes 33554560 | tf_op jit(solution)/shard_map/gather | solution.py:19
  79.2 13.5 %bitcast_reduce_fusion.5 = (f32[16,256]{1,0:T(8,128)S(1)}, f32[16,2,256,256]{3,2,1,0:T(8,128)}) fusion(f32[16,2,256]{2,1,0:T(2,128)S(1)} %reshape.108, pred[16,2]{1,0:T(8,128)(4,1)S(1)} %iota_compare_fusion, bf16[16,2,256,1024]{3,2,1,0:T(8,128)(2,1)} %bitcast.58, bf16[16,256,1024,1]{2,1,3,0:T(8,128)(2,1)} %bitcast.63), kind=kOutput, calls=%fused_computation.28 | convolution fusion | flops 4303351808 | bytes 33603616 | tf_op jit(solution)/shard_map/rad,rkbd->rkab/dot_general | solution.py:20
  92.6 18.7 %pmax.42 = f32[16,256]{1,0:T(8,128)S(1)} all-reduce(f32[16,256]{1,0:T(8,128)S(1)} %get-tuple-element.2), channel_id=1, replica_groups=mesh['row'=8,'col'=4] {'col'}, use_global_device_ids=true, to_apply=%region_1.2 | all-reduce | flops 4096 | bytes 32768 | tf_op jit(solution)/shard_map/pmax | solution.py:44
  111.4 4.6 %fusion.11 = f32[16,256]{1,0:T(8,128)S(1)} fusion(f32[16,256]{1,0:T(8,128)S(1)} %pmax.42, f32[16,2,256]{2,1,0:T(2,128)S(1)} %reshape.108, pred[16,2]{1,0:T(8,128)(4,1)S(1)} %iota_compare_fusion, f32[16,2,256,256]{3,2,1,0:T(8,128)} %get-tuple-element.3), kind=kLoop, calls=%fused_computation.30 | loop fusion | flops 10481664 | bytes 8454176 | tf_op jit(solution)/shard_map/reduce_sum | solution.py:45
  116.0 15.5 %psum.42 = f32[16,256]{1,0:T(8,128)S(1)} all-reduce(f32[16,256]{1,0:T(8,128)S(1)} %fusion.11), channel_id=1, replica_groups=mesh['row'=8,'col'=4] {'col'}, use_global_device_ids=true, to_apply=%region_3.4 | all-reduce | flops 4096 | bytes 32768 | tf_op jit(solution)/shard_map/psum | solution.py:46
  131.6 4.7 %bitcast_reduce_fusion.4 = f32[16,2,256]{2,1,0:T(2,128)S(1)} fusion(f32[16,256]{1,0:T(8,128)S(1)} %log_subtract_fusion.4, pred[16,2]{1,0:T(8,128)(4,1)S(1)} %iota_compare_fusion, f32[16,2,256,256]{3,2,1,0:T(8,128)} %get-tuple-element.3), kind=kLoop, calls=%fused_computation.24 | loop fusion | flops 8380416 | bytes 8437792 | tf_op jit(solution)/shard_map/reduce_max | solution.py:50
  136.4 22.3 %pmax.43 = f32[16,256]{1,0:T(8,128)S(1)} all-reduce(f32[16,256]{1,0:T(8,128)S(1)} %select_reduce_fusion.5), channel_id=1, replica_groups=mesh['row'=8,'col'=4] {'row'}, use_global_device_ids=true, to_apply=%region_6.7 | all-reduce | flops 4096 | bytes 32768 | tf_op jit(solution)/shard_map/pmax | solution.py:54
  159.3 5.1 %fusion.9 = f32[16,2,256]{2,1,0:T(2,128)S(1)} fusion(f32[16,2,256]{2,1,0:T(2,128)S(1)} %reshape.116, f32[16,256]{1,0:T(8,128)S(1)} %log_subtract_fusion.4, pred[16,2]{1,0:T(8,128)(4,1)S(1)} %iota_compare_fusion, f32[16,2,256,256]{3,2,1,0:T(8,128)} %get-tuple-element.3), kind=kLoop, calls=%fused_computation.26 | loop fusion | flops 10477568 | bytes 8470560 | tf_op jit(solution)/shard_map/reduce_sum | solution.py:56
  164.6 22.3 %psum.43 = f32[16,256]{1,0:T(8,128)S(1)} all-reduce(f32[16,256]{1,0:T(8,128)S(1)} %select_reduce_fusion.4), channel_id=1, replica_groups=mesh['row'=8,'col'=4] {'row'}, use_global_device_ids=true, to_apply=%region_9.10 | all-reduce | flops 4096 | bytes 32768 | tf_op jit(solution)/shard_map/psum | solution.py:58
  187.6 4.4 %bitcast_reduce_fusion.3 = f32[16,256]{1,0:T(8,128)S(1)} fusion(f32[16,2,256]{2,1,0:T(2,128)S(1)} %reshape.124, pred[16,2]{1,0:T(8,128)(4,1)S(1)} %iota_compare_fusion, f32[16,2,256,256]{3,2,1,0:T(8,128)} %get-tuple-element.3), kind=kLoop, calls=%fused_computation.20 | loop fusion | flops 8384512 | bytes 8437792 | tf_op jit(solution)/shard_map/reduce_max | solution.py:43
  192.0 16.3 %pmax.44 = f32[16,256]{1,0:T(8,128)S(1)} all-reduce(f32[16,256]{1,0:T(8,128)S(1)} %bitcast_reduce_fusion.3), channel_id=1, replica_groups=mesh['row'=8,'col'=4] {'col'}, use_global_device_ids=true, to_apply=%region_11.12 | all-reduce | flops 4096 | bytes 32768 | tf_op jit(solution)/shard_map/pmax | solution.py:44
  208.3 4.6 %fusion.7 = f32[16,256]{1,0:T(8,128)S(1)} fusion(f32[16,256]{1,0:T(8,128)S(1)} %pmax.44, f32[16,2,256]{2,1,0:T(2,128)S(1)} %reshape.124, pred[16,2]{1,0:T(8,128)(4,1)S(1)} %iota_compare_fusion, f32[16,2,256,256]{3,2,1,0:T(8,128)} %get-tuple-element.3), kind=kLoop, calls=%fused_computation.22 | loop fusion | flops 10481664 | bytes 8454176 | tf_op jit(solution)/shard_map/reduce_sum | solution.py:45
  213.0 15.5 %psum.44 = f32[16,256]{1,0:T(8,128)S(1)} all-reduce(f32[16,256]{1,0:T(8,128)S(1)} %fusion.7), channel_id=1, replica_groups=mesh['row'=8,'col'=4] {'col'}, use_global_device_ids=true, to_apply=%region_13.14 | all-reduce | flops 4096 | bytes 32768 | tf_op jit(solution)/shard_map/psum | solution.py:46
  228.5 4.7 %bitcast_reduce_fusion.2 = f32[16,2,256]{2,1,0:T(2,128)S(1)} fusion(f32[16,256]{1,0:T(8,128)S(1)} %log_subtract_fusion.2, pred[16,2]{1,0:T(8,128)(4,1)S(1)} %iota_compare_fusion, f32[16,2,256,256]{3,2,1,0:T(8,128)} %get-tuple-element.3), kind=kLoop, calls=%fused_computation.16 | loop fusion | flops 8380416 | bytes 8437792 | tf_op jit(solution)/shard_map/reduce_max | solution.py:50
  233.3 22.3 %pmax.45 = f32[16,256]{1,0:T(8,128)S(1)} all-reduce(f32[16,256]{1,0:T(8,128)S(1)} %select_reduce_fusion.3), channel_id=1, replica_groups=mesh['row'=8,'col'=4] {'row'}, use_global_device_ids=true, to_apply=%region_16.17 | all-reduce | flops 4096 | bytes 32768 | tf_op jit(solution)/shard_map/pmax | solution.py:54
  256.3 5.1 %fusion.5 = f32[16,2,256]{2,1,0:T(2,128)S(1)} fusion(f32[16,2,256]{2,1,0:T(2,128)S(1)} %reshape.132, f32[16,256]{1,0:T(8,128)S(1)} %log_subtract_fusion.2, pred[16,2]{1,0:T(8,128)(4,1)S(1)} %iota_compare_fusion, f32[16,2,256,256]{3,2,1,0:T(8,128)} %get-tuple-element.3), kind=kLoop, calls=%fused_computation.18 | loop fusion | flops 10477568 | bytes 8470560 | tf_op jit(solution)/shard_map/reduce_sum | solution.py:56
  261.6 22.3 %psum.45 = f32[16,256]{1,0:T(8,128)S(1)} all-reduce(f32[16,256]{1,0:T(8,128)S(1)} %select_reduce_fusion.2), channel_id=1, replica_groups=mesh['row'=8,'col'=4] {'row'}, use_global_device_ids=true, to_apply=%region_19.20 | all-reduce | flops 4096 | bytes 32768 | tf_op jit(solution)/shard_map/psum | solution.py:58
  284.5 4.4 %bitcast_reduce_fusion.1 = f32[16,256]{1,0:T(8,128)S(1)} fusion(f32[16,2,256]{2,1,0:T(2,128)S(1)} %reshape.140, pred[16,2]{1,0:T(8,128)(4,1)S(1)} %iota_compare_fusion, f32[16,2,256,256]{3,2,1,0:T(8,128)} %get-tuple-element.3), kind=kLoop, calls=%fused_computation.12 | loop fusion | flops 8384512 | bytes 8437792 | tf_op jit(solution)/shard_map/reduce_max | solution.py:43
  288.9 16.3 %pmax.46 = f32[16,256]{1,0:T(8,128)S(1)} all-reduce(f32[16,256]{1,0:T(8,128)S(1)} %bitcast_reduce_fusion.1), channel_id=1, replica_groups=mesh['row'=8,'col'=4] {'col'}, use_global_device_ids=true, to_apply=%region_21.22 | all-reduce | flops 4096 | bytes 32768 | tf_op jit(solution)/shard_map/pmax | solution.py:44
  305.3 4.6 %fusion.3 = f32[16,256]{1,0:T(8,128)S(1)} fusion(f32[16,256]{1,0:T(8,128)S(1)} %pmax.46, f32[16,2,256]{2,1,0:T(2,128)S(1)} %reshape.140, pred[16,2]{1,0:T(8,128)(4,1)S(1)} %iota_compare_fusion, f32[16,2,256,256]{3,2,1,0:T(8,128)} %get-tuple-element.3), kind=kLoop, calls=%fused_computation.14 | loop fusion | flops 10481664 | bytes 8454176 | tf_op jit(solution)/shard_map/reduce_sum | solution.py:45
  309.9 15.5 %psum.46 = f32[16,256]{1,0:T(8,128)S(1)} all-reduce(f32[16,256]{1,0:T(8,128)S(1)} %fusion.3), channel_id=1, replica_groups=mesh['row'=8,'col'=4] {'col'}, use_global_device_ids=true, to_apply=%region_23.24 | all-reduce | flops 4096 | bytes 32768 | tf_op jit(solution)/shard_map/psum | solution.py:46
  325.4 4.7 %bitcast_reduce_fusion = f32[16,2,256]{2,1,0:T(2,128)S(1)} fusion(f32[16,256]{1,0:T(8,128)S(1)} %log_subtract_fusion, pred[16,2]{1,0:T(8,128)(4,1)S(1)} %iota_compare_fusion, f32[16,2,256,256]{3,2,1,0:T(8,128)} %get-tuple-element.3), kind=kLoop, calls=%fused_computation.8 | loop fusion | flops 8380416 | bytes 8437792 | tf_op jit(solution)/shard_map/reduce_max | solution.py:50
  330.3 22.3 %pmax.47 = f32[16,256]{1,0:T(8,128)S(1)} all-reduce(f32[16,256]{1,0:T(8,128)S(1)} %select_reduce_fusion.1), channel_id=1, replica_groups=mesh['row'=8,'col'=4] {'row'}, use_global_device_ids=true, to_apply=%region_26.27 | all-reduce | flops 4096 | bytes 32768 | tf_op jit(solution)/shard_map/pmax | solution.py:54
  353.2 5.1 %fusion.1 = f32[16,2,256]{2,1,0:T(2,128)S(1)} fusion(f32[16,2,256]{2,1,0:T(2,128)S(1)} %reshape.148, f32[16,256]{1,0:T(8,128)S(1)} %log_subtract_fusion, pred[16,2]{1,0:T(8,128)(4,1)S(1)} %iota_compare_fusion, f32[16,2,256,256]{3,2,1,0:T(8,128)} %get-tuple-element.3), kind=kLoop, calls=%fused_computation.10 | loop fusion | flops 10477568 | bytes 8470560 | tf_op jit(solution)/shard_map/reduce_sum | solution.py:56
  358.5 22.3 %psum.47 = f32[16,256]{1,0:T(8,128)S(1)} all-reduce(f32[16,256]{1,0:T(8,128)S(1)} %select_reduce_fusion), channel_id=1, replica_groups=mesh['row'=8,'col'=4] {'row'}, use_global_device_ids=true, to_apply=%region_29.30 | all-reduce | flops 4096 | bytes 32768 | tf_op jit(solution)/shard_map/psum | solution.py:58
  (34 shorter events, 6.2 us)
Async XLA Ops:
  7.2 61.4 %all-gather.2.cloned.1.call-start = ((), (), s32[]{:S(2)}) async-start(), calls=%async_computation | async-start | bytes 9437184 | tf_op jit(solution)/shard_map/all_gather | solution.py:37
Sparse Core Ops, SparseCore 0:
  9.9 58.6 all-gather.1
where the time goes:
time: 390 us; the launch traced here: 389 us
  blocking collectives  232 us (59%)
  waiting for transfers between devices  56.8 us (15%)
  other arithmetic  54.5 us (14%)
  local copies, waits for them, and re-layouts  18 us (5%)
  between operations  14.3 us (4%)
  matrix products  13.5 us (3%)
    pmax x3, blocking collectives, on_device(): col_high = lax.pmax(local_top, 'row')  66.9 us
    psum x3, blocking collectives, on_device(): col_total = lax.psum(col_sum, 'row')  66.9 us
    all_gather x1, waiting for transfers between devices, on_device(): lax.all_gather(target_points, 'row', axis=1, tiled=True)  56.1 us
    pmax x3, blocking collectives, on_device(): highest = lax.pmax(row_top, 'col')  51.4 us
    psum x3, blocking collectives, on_device(): total = lax.psum(local_sum, 'col')  46.6 us
    reduce_sum x3, other arithmetic, on_device(): sums = jnp.sum(jnp.exp(columns - slot_ref[:, :, None, :]), axis=2)  15.4 us
    reduce_max x3, other arithmetic, on_device(): slot_top = jnp.max(columns, axis=2)  14 us
    reduce_sum x3, other arithmetic, on_device(): jnp.sum(jnp.exp(scores - highest[:, None, :, None]), axis=(1, 3))  13.9 us
  transfers between devices with their start and end apart: 1, of which 1 were waited for; matrix products, arithmetic and copies ran while one was open for 1% of the time, Pallas kernels for 0%

commit v1 on v0

v1 whole, which is shorter than its diff:
```python
import functools
import math

import jax
import jax.numpy as jnp
from jax import lax
from jax.experimental import pallas as pl
from jax.experimental.pallas import tpu as pltpu
from jax.sharding import PartitionSpec as P

TILE = 256
LANES = 128
STRIP = 32
HALF = 64
LOW = -1e30
FLOOR = -1e29
LEAST = 1e-15
LOG2_E = math.log2(math.e)
LN_2 = math.log(2.0)

VMEM = pltpu.MemorySpace.VMEM
SMEM = pltpu.MemorySpace.SMEM
NT = (((1,), (1,)), ((), ()))


def kernel_call(body, outs, operands, scratch, name, final=False, aliases=None):
    specs = []
    placed = []
    for x in operands:
        if x.dtype == jnp.int32:
            specs.append(pl.BlockSpec(memory_space=SMEM))
            placed.append(x)
        else:
            specs.append(pl.BlockSpec(memory_space=VMEM))
            placed.append(pltpu.with_memory_space_constraint(x, VMEM))
    return pl.pallas_call(
        body,
        out_shape=[
            (jax.ShapeDtypeStruct if final else VMEM)(shape, jnp.float32) for shape in outs
        ],
        in_specs=specs,
        out_specs=[pl.BlockSpec(memory_space=VMEM)] * len(outs),
        input_output_aliases=aliases or {},
        scratch_shapes=[pltpu.VMEM(shape, jnp.float32) for shape in scratch],
        cost_estimate=pl.CostEstimate(flops=1 << 13, bytes_accessed=1 << 10, transcendentals=0),
        compiler_params=pltpu.CompilerParams(vmem_limit_bytes=8 << 20),
        name=name,
    )(*placed)


def to_rows(columns, tiles):
    return columns.T[:tiles]


def to_columns(rows):
    tiles = rows.shape[0]
    padded = jnp.concatenate([rows, jnp.zeros((LANES - tiles, TILE), jnp.float32)], axis=0)
    return padded.T


def put_lanes(ref, start, columns):
    rows = pl.ds(start, STRIP)
    lane = lax.broadcasted_iota(jnp.int32, (STRIP, LANES), 1)
    value = ref[rows, :]
    for at, column in columns.items():
        value = jnp.where(lane == at, column, value)
    ref[rows, :] = value


def halves(x, op):
    return op(x[:, :LANES], x[:, LANES:])


def from_flat(ref):
    step = TILE // LANES
    parts = [ref[pl.ds(h, ref.shape[0] // step, stride=step), :] for h in range(step)]
    return jnp.concatenate(parts, axis=1)


def put_flat(ref, value):
    for h in range(TILE // LANES):
        ref[pl.ds(h, value.shape[0], stride=TILE // LANES), :] = value[:, h * LANES : (h + 1) * LANES]


def score_kernel(distances, first, last, scale, *refs):
    pieces = len(distances)
    index, count, source = refs[:3]
    targets = refs[3 : 3 + pieces]
    refs = refs[3 + pieces :]
    if not first:
        before, *refs = refs
    score, *outs, columns = refs
    tiles, slots = score.shape[:2]
    me = lax.axis_index("row")
    offset = [
        (me ^ jnp.where((me & 1) == 0, zero, one)) * target.shape[1]
        for (zero, one), target in zip(distances, targets)
    ]
    if targets[0].shape[1] == source.shape[1]:
        offset = [0]
    if first:
        name_slots(index, count, outs[-1], slots)

    def products(t):
        rows = pl.ds(t * TILE if last else pl.multiple_of(t * TILE, TILE), TILE)
        left = [
            source[rows, pl.ds(pl.multiple_of(offset[k], targets[k].shape[1]), targets[k].shape[1])]
            for k in range(pieces)
        ]
        left = jnp.concatenate(left, axis=1) if pieces > 1 else left[0]
        for s in range(slots):
            chosen = pl.ds(pl.multiple_of(index[s, t] * TILE, TILE), TILE)
            right = [targets[k][chosen, :] for k in range(pieces)]
            right = jnp.concatenate(right, axis=1) if pieces > 1 else right[0]
            block = lax.dot_general(left, right, NT, preferred_element_type=jnp.float32)
            if not first:
                block = before[t, s] + block
            if last:
                block = block * scale
                if s > 0:
                    block = jnp.where(s < count[0, t], block, LOW)
            score[t, s] = block

    def statistics(t):
        for r in range(0, TILE, STRIP):
            blocks = [score[t, s, r : r + STRIP] for s in range(slots)]
            top = halves(functools.reduce(jnp.maximum, blocks), jnp.maximum)
            top = jnp.max(top, axis=1, keepdims=True)
            total = functools.reduce(jnp.add, [jnp.exp2(block - top) for block in blocks])
            total = jnp.sum(halves(total, jnp.add), axis=1, keepdims=True)
            put_lanes(columns, r, {t: top, HALF + t: total})

    if last:
        for t in range(tiles + 1):
            if t < tiles:
                products(t)
            if t > 0:
                statistics(t - 1)
        stats = columns[...].T
        outs[0][0] = stats[:tiles]
        outs[0][1] = stats[HALF : HALF + tiles]
    else:
        lax.fori_loop(0, tiles, lambda t, carry: (products(t), carry)[1], 0, unroll=4)
    if not first and not last:
        outs[0][...] = jnp.zeros(outs[0].shape, jnp.float32)


def name_slots(index, count, names, slots):
    for k in range(names.shape[0]):
        t, s = divmod(k, slots)
        name = jnp.where(s < count[0, t], index[s, t], -1).astype(jnp.float32)
        names[k : k + 1, :] = jnp.full((1, TILE), name, jnp.float32)


def to_slots(names, rows):
    taken = jnp.zeros(names.shape, jnp.float32)
    for u in range(rows.shape[0]):
        taken = jnp.where(names == u, rows[u : u + 1, :], taken)
    return taken


def to_targets(names, values, out, op, empty):
    for u in range(out.shape[0]):
        out[u : u + 1, :] = op(jnp.where(names == u, values, empty), axis=0, keepdims=True)


def merge(refs):
    top = functools.reduce(jnp.maximum, [ref[0] for ref in refs])
    total = functools.reduce(jnp.add, [ref[1] * jnp.exp2(ref[0] - top) for ref in refs])
    return top, total


def total_of(refs):
    return functools.reduce(jnp.add, [ref[...] for ref in refs])


def exp_kernel(score, stats, kernel, columns):
    tiles, slots = kernel.shape[:2]
    columns[...] = to_columns(stats[0])
    for t in range(tiles):
        for r in range(0, TILE, STRIP):
            column = columns[r : r + STRIP, t : t + 1]
            for s in range(slots):
                kernel[t, s, r : r + STRIP] = jnp.exp2(score[t, s, r : r + STRIP] - column)


def slot_sums(kernel, columns, sums):
    tiles, slots = kernel.shape[:2]
    for t in range(tiles):
        total = [None] * slots
        for r in range(0, TILE, STRIP):
            column = columns[r : r + STRIP, t : t + 1]
            for s in range(slots):
                block = kernel[t, s, r : r + STRIP] * column
                total[s] = block if r == 0 else total[s] + block
        for s in range(slots):
            k = t * slots + s
            sums[k : k + 1, :] = jnp.sum(total[s], axis=0, keepdims=True)


def first_column_kernel(parts, names, score, before, mass, *refs):
    gathered = refs[:parts]
    kernel, stats, tops, potential, factor, columns, sums = refs[parts:]
    tiles, slots = kernel.shape[:2]
    top, total = merge(gathered)
    row = LOG2_E * (jnp.log(from_flat(mass)) - jnp.log(total)) - top
    potential[...] = row
    factor[...] = jnp.exp2(gathered[0][0] + row)
    columns[...] = to_columns(factor[...])
    slot_sums(before, columns, sums)
    tops[...] = jnp.zeros(tops.shape, jnp.float32)
    least = jnp.min(jnp.where(names[...] >= 0, sums[...], 1.0))

    @pl.when(least < LEAST)
    def _():
        factor[...] = jnp.ones(factor.shape, jnp.float32)
        columns[...] = to_columns(row)
        for t in range(tiles):
            best = [None] * slots
            for r in range(0, TILE, STRIP):
                column = columns[r : r + STRIP, t : t + 1]
                for s in range(slots):
                    block = score[t, s, r : r + STRIP] + column
                    best[s] = block if r == 0 else jnp.maximum(best[s], block)
            best = [jnp.maximum(jnp.max(x, axis=0, keepdims=True), FLOOR) for x in best]
            total = [None] * slots
            for r in range(0, TILE, STRIP):
                column = columns[r : r + STRIP, t : t + 1]
                for s in range(slots):
                    block = jnp.exp2(score[t, s, r : r + STRIP] + column - best[s])
                    kernel[t, s, r : r + STRIP] = block
                    total[s] = block if r == 0 else total[s] + block
            for s in range(slots):
                k = t * slots + s
                tops[k : k + 1, :] = best[s]
                sums[k : k + 1, :] = jnp.sum(total[s], axis=0, keepdims=True)

    named = names[...]
    to_targets(named, tops[...], stats.at[0], jnp.max, FLOOR)
    change = jnp.exp2(tops[...] - to_slots(named, stats[0]))
    to_targets(named, sums[...] * change, stats.at[1], jnp.sum, 0.0)


def row_sums(kernel, weights, factor, out, columns):
    tiles, slots = kernel.shape[:2]
    for t in range(tiles):
        weight = [weights[t * slots + s : t * slots + s + 1, :] for s in range(slots)]
        for r in range(0, TILE, STRIP):
            blocks = [kernel[t, s, r : r + STRIP] * weight[s] for s in range(slots)]
            total = halves(functools.reduce(jnp.add, blocks), jnp.add)
            put_lanes(columns, r, {t: jnp.sum(total, axis=1, keepdims=True)})
    out[...] = to_rows(columns[...], tiles) * factor[...]


def first_row_kernel(parts, names, kernel, mass, factor, tops, *refs):
    gathered = refs[:parts]
    out, potential, weights, columns = refs[parts:]
    top, total = merge(gathered)
    value = LOG2_E * (jnp.log(from_flat(mass)) - jnp.log(total)) - top
    potential[...] = value
    weights[...] = jnp.exp2(tops[...] + to_slots(names[...], value))
    row_sums(kernel, weights, factor, out, columns)


def column_kernel(parts, last, names, kernel, mass, factor, weights, *refs):
    if last:
        start, *refs = refs
    gathered = refs[:parts]
    out, *potential, columns, sums = refs[parts:]
    scaling = from_flat(mass) / total_of(gathered)
    columns[...] = to_columns(scaling * factor[...])
    slot_sums(kernel, columns, sums)
    to_targets(names[...], sums[...] * weights[...], out, jnp.sum, 0.0)
    if last:
        put_flat(potential[0], LN_2 * start[...] + jnp.log(scaling))


def row_kernel(parts, names, kernel, mass, factor, weights, *refs):
    gathered = refs[:parts]
    out, columns, scaled = refs[parts:]
    scaling = from_flat(mass) / total_of(gathered)
    scaled[...] = weights[...] * to_slots(names[...], scaling)
    row_sums(kernel, scaled, factor, out, columns)


def last_kernel(parts, mass, start, *refs):
    scaling = from_flat(mass) / total_of(refs[:parts])
    put_flat(refs[parts], LN_2 * start[...] + jnp.log(scaling))


def permute(x, axis, n, partner):
    return lax.ppermute(x, axis, [(i, partner(i)) for i in range(n)])


def swap(x, axis, n, mask):
    return permute(x, axis, n, lambda i: i ^ mask)


def merged(pairs):
    top = functools.reduce(jnp.maximum, [pair[0] for pair in pairs])
    total = functools.reduce(jnp.add, [pair[1] * jnp.exp2(pair[0] - top) for pair in pairs])
    here = lax.broadcasted_iota(jnp.int32, pairs[0].shape, 0)
    return jnp.where(here == 0, top[None], total[None])


def exchange(x, axis, sizes, join, orders=((3, 1), (2, 3), (1, 2))):
    n_row, n_col = sizes
    n = n_row if axis == "row" else n_col
    if n & (n - 1):
        return [lax.all_gather(x, axis)[k] for k in range(n)]
    low = 1
    while n // low not in (1, 4):
        x = join([x, swap(x, axis, n, low)])
        low *= 2
    if low == n:
        return [x]
    mixed = axis == "col" or low > 1
    parts = [x]
    for even, odd in orders:
        pairs = []
        for row in range(n_row):
            for col in range(n_col):
                mask = low * (odd if mixed and row & 1 else even)
                to = (row ^ mask, col) if axis == "row" else (row, col ^ mask)
                pairs.append((row * n_col + col, to[0] * n_col + to[1]))
        parts.append(lax.ppermute(x, ("row", "col"), pairs))
    return parts


def first_way(i):
    return i ^ (4 if i & 1 else 2)


def second_way(i):
    return i ^ (2 if i & 1 else 4)


def scores_by_chip(score, target, n):
    first = permute(target, "row", n, first_way)
    part, names = score(None, [(target, (0, 0))], False)
    later, names = lax.optimization_barrier((target, names))
    second = permute(later, "row", n, second_way)
    first, part, names = lax.optimization_barrier((first, part, names))
    half = first.shape[0] // 2
    early, late = (permute(part, "row", n, second_way) for part in (first[:half], first[half:]))
    sibling = swap(target, "row", n, 1)
    first_sibling = swap(first, "row", n, 1)
    part, second = lax.optimization_barrier((part, second))
    pieces = [(sibling, (1, 1)), (first, (2, 4)), (first_sibling, (5, 3))]
    part, mark = score(part, pieces, False)
    second, early, part, _ = lax.optimization_barrier((second, early, part, mark))
    second_sibling = swap(second, "row", n, 1)
    early_sibling = swap(early, "row", n, 1)
    late, early_sibling = lax.optimization_barrier((late, early_sibling))
    corner = jnp.concatenate([early, late], axis=0)
    corner_sibling = jnp.concatenate([early_sibling, swap(late, "row", n, 1)], axis=0)
    pieces = [(second, (4, 2)), (second_sibling, (3, 5)), (corner, (6, 6)), (corner_sibling, (7, 7))]
    return [*score(part, pieces, True), names]


def on_device(n_row, n_col, source, target, source_mass, target_mass, tile_index, tile_count):
    tiles = source.shape[0] // TILE
    col_tiles = target.shape[0] // TILE
    slots = tile_index.shape[1]
    scale = LOG2_E / math.sqrt(source.shape[1])
    pairs = tiles * slots * TILE * TILE
    grid = (tiles, slots, TILE, TILE)
    source_rows, target_rows = (tiles, TILE), (col_tiles, TILE)
    a = source_mass.reshape(-1, LANES)
    b = target_mass.reshape(-1, LANES)
    index, count = tile_index.T, tile_count.T
    slot_rows = (tiles * slots, TILE)
    columns = (TILE, LANES)
    sizes = (n_row, n_col)

    def score(before, pieces, last):
        operands = [index, count, source, *[piece for piece, _ in pieces]]
        outs = [grid]
        if last:
            outs.append((2, *source_rows))
        if before is None:
            outs.append(slot_rows)
        else:
            operands.append(before)
            if not last:
                outs.append((8, LANES))
        distances = [k for _, k in pieces]
        return kernel_call(
            functools.partial(score_kernel, distances, before is None, last, scale),
            outs,
            operands,
            [columns],
            f"score_{len(pieces)}_{last}",
        )

    if n_row == 8 and target.shape[1] % LANES == 0:
        scores, stats, names = scores_by_chip(score, target, n_row)
    else:
        whole = lax.all_gather(target, "row", axis=1, tiled=True)
        scores, stats, names = score(None, [(whole, (0, 0))], True)

    def phase(body, name, outs, operands, parts, scratch=(), final=False, aliases=None):
        body = functools.partial(body, len(parts))
        return kernel_call(body, outs, [*operands, *parts], scratch, name, final, aliases)

    def added(values):
        return functools.reduce(jnp.add, values)

    flat = (tiles * TILE // LANES, LANES)
    parts = exchange(stats, "col", sizes, merged, ((1, 2), (3, 1), (2, 3)))
    (kernel,) = kernel_call(exp_kernel, [grid], [scores, stats], [columns], "exps")
    kernel, stats, tops, f_first, factor = phase(
        first_column_kernel,
        "column_0",
        [grid, (2, *target_rows), slot_rows, source_rows, source_rows],
        [names, scores, kernel, a],
        parts,
        [columns, slot_rows],
        aliases={2: 0},
    )
    parts = exchange(stats, "row", sizes, merged)
    sums, g_first, weights = phase(
        first_row_kernel,
        "row_1",
        [source_rows, target_rows, slot_rows],
        [names, kernel, b, factor, tops],
        parts,
        [columns],
    )
    parts = exchange(sums, "col", sizes, added)
    (sums,) = phase(
        lambda n, *refs: column_kernel(n, False, *refs),
        "column_1",
        [target_rows],
        [names, kernel, a, factor, weights],
        parts,
        [columns, slot_rows],
    )
    parts = exchange(sums, "row", sizes, added)
    (sums,) = phase(
        row_kernel,
        "row_2",
        [source_rows],
        [names, kernel, b, factor, weights],
        parts,
        [columns, slot_rows],
    )
    parts = exchange(sums, "col", sizes, added)
    sums, f_last = phase(
        lambda n, *refs: column_kernel(n, True, *refs),
        "column_2",
        [target_rows, flat],
        [names, kernel, a, factor, weights, f_first],
        parts,
        [columns, slot_rows],
    )
    parts = exchange(sums, "row", sizes, added)
    (g_last,) = phase(
        last_kernel, "last", [(col_tiles * TILE // LANES, LANES)], [b, g_first], parts, final=True
    )
    return (f_last.reshape(-1), g_last.reshape(-1))


def solution(mesh):
    placed = (P("row", None), P("col", "row"), P("row"), P("col"), P("row", "col"), P("row", "col"))
    return jax.shard_map(
        functools.partial(on_device, mesh.shape["row"], mesh.shape["col"]),
        mesh=mesh,
        in_specs=placed,
        out_specs=(P("row"), P("col")),
        check_vma=False,
    )
```

time: 390 us -> 95.9 us (0.25)
  blocking collectives: 232 us -> 0 us
  other arithmetic: 54.5 us -> 0.24 us
  starting transfers between devices: 0.04 us -> 33.9 us
  waiting for transfers between devices: 56.8 us -> 36.8 us
  Pallas kernels: 0 us -> 17.3 us
  between operations: 14.3 us -> 0.79 us
  matrix products: 13.5 us -> 0 us
  local copies, waits for them, and re-layouts: 18 us -> 6.63 us
    pmax x6 -> x0, blocking collectives: 118 us -> none  [the longest x3 66.9 us: on_device(): col_high = lax.pmax(local_top, 'row')]
    psum x6 -> x0, blocking collectives: 114 us -> none  [the longest x3 66.9 us: on_device(): col_total = lax.psum(col_sum, 'row')]
    all_gather x1 -> x0, waiting for transfers between devices: 56.1 us -> none  [on_device(): lax.all_gather(target_points, 'row', axis=1, tiled=True)]
    ppermute x0 -> x30, waiting for transfers between devices: none -> 36.8 us  [the longest x12 21.1 us: permute(): return lax.ppermute(x, axis, [(i, partner(i)) for i in range(n)])]
    ppermute x0 -> x30, starting transfers between devices: none -> 33.9 us  [the longest x18 24.2 us: exchange(): parts.append(lax.ppermute(x, ('row', 'col'), pairs))]
    reduce_sum x9 -> x0, other arithmetic: 29.7 us -> none  [the longest x3 15.4 us: on_device(): sums = jnp.sum(jnp.exp(columns - slot_ref[:, :, None, :]), axis=2)]
    reduce_max x8 -> x0, other arithmetic: 23.2 us -> none  [the longest x3 14 us: on_device(): slot_top = jnp.max(columns, axis=2)]
    pallas_call x0 -> x10, Pallas kernels: none -> 17.3 us  [kernel_call(): pl.pallas_call(body, out_shape=[(jax.ShapeDtypeStruct if final else VMEM)...]
  transfers between devices with their start and end apart: 1 -> 30, of which waited for: 1 -> 23; matrix products, arithmetic and copies ran while one was open for 1% -> 1% of each run, Pallas kernels for 0% -> 8%
where the time goes in v1:
time: 95.9 us; the launch traced here: 95.7 us
  waiting for transfers between devices  36.8 us (38%)
  starting transfers between devices  33.9 us (35%)
  Pallas kernels  17.3 us (18%)
  local copies, waits for them, and re-layouts  6.63 us (7%)
    ppermute x18, starting transfers between devices, exchange(): parts.append(lax.ppermute(x, ('row', 'col'), pairs))  24.2 us
    ppermute x12, waiting for transfers between devices, permute(): return lax.ppermute(x, axis, [(i, partner(i)) for i in range(n)])  21.1 us
    pallas_call x10, Pallas kernels, kernel_call(): pl.pallas_call(body, out_shape=[(jax.ShapeDtypeStruct if final else VMEM)...  17.3 us
    ppermute x18, waiting for transfers between devices, exchange(): parts.append(lax.ppermute(x, ('row', 'col'), pairs))  15.8 us
    ppermute x12, starting transfers between devices, permute(): return lax.ppermute(x, axis, [(i, partner(i)) for i in range(n)])  9.77 us
    unnamed x19, local copies, waits for them, and re-layouts  6.56 us
  transfers between devices with their start and end apart: 30, of which 23 were waited for; matrix products, arithmetic and copies ran while one was open for 1% of the time, Pallas kernels for 8%

profile of v1, /device:TPU:0, one launch (start us, length us, event | category | flops | bytes accessed | tf_op | source)
XLA Modules:
  0.0 95.7 jit_solution(10812923969238934358)
XLA Ops:
  0.7 3.0 %collective-permute-start = (bf16[4096,128]{1,0:T(8,128)(2,1)}, bf16[4096,128]{1,0:T(8,128)(2,1)S(1)}, u32[]{:S(2)}, u32[]{:S(2)}) collective-permute-start(bf16[4096,128]{1,0:T(8,128)(2,1)} %refs_3_.1), channel_id=1, source_target_pairs={{0,8},{4,20},{8,0},{12,28},{16,24},{20,4},{24,16},{28,12},{1,9},{5... | collective-permute-start | bytes 3145736 | tf_op jit(solution)/shard_map/ppermute | solution.py:292
  3.7 3.4 %copy-done = bf16[4096,1024]{1,0:T(8,128)(2,1)S(1)} copy-done((bf16[4096,1024]{1,0:T(8,128)(2,1)S(1)}, bf16[4096,1024]{1,0:T(8,128)(2,1)}, u32[]{:S(2)}) %copy-start) | copy-done | bytes 8388632
  7.0 1.2 %copy-done.2 = bf16[4096,128]{1,0:T(8,128)(2,1)S(1)} copy-done((bf16[4096,128]{1,0:T(8,128)(2,1)S(1)}, bf16[4096,128]{1,0:T(8,128)(2,1)}, u32[]{:S(2)}) %copy-start.2) | copy-done | bytes 1048600
  9.6 2.4 %score_1_False.1 = (f32[16,2,256,256]{3,2,1,0:T(8,128)S(1)}, f32[32,256]{1,0:T(8,128)S(1)}) custom-call(s32[2,16]{1,0:T(2,128)S(1)} %bitcast.17, s32[1,16]{1,0:T(1,128)S(1)} %bitcast.20, bf16[4096,1024]{1,0:T(8,128)(2,1)S(1)} %copy-done, bf16[4096,128]{1,0:T(8,128)(2,1)S(1)} %copy-done.2), custom_call_target="tpu_custom_call" | custom-call | flops 8192 | bytes 1024 | tf_op jit(solution)/shard_map/score_1_False/pallas_call | solution.py:36
  12.0 1.6 %collective-permute-start.1 = (bf16[4096,128]{1,0:T(8,128)(2,1)S(1)}, bf16[4096,128]{1,0:T(8,128)(2,1)S(1)}, u32[]{:S(2)}, u32[]{:S(2)}) collective-permute-start(bf16[4096,128]{1,0:T(8,128)(2,1)S(1)} %copy-done.2), channel_id=1, source_target_pairs={{0,16},{4,12},{8,24},{12,4},{16,0},{20,28},{24,8},{28,20},{1,17},{... | collective-permute-start | bytes 3145736 | tf_op jit(solution)/shard_map/ppermute | solution.py:292
  13.6 5.6 %collective-permute-done.refs_4_ = bf16[4096,128]{1,0:T(8,128)(2,1)S(1)} collective-permute-done((bf16[4096,128]{1,0:T(8,128)(2,1)}, bf16[4096,128]{1,0:T(8,128)(2,1)S(1)}, u32[]{:S(2)}, u32[]{:S(2)}) %collective-permute-start) | collective-permute-done | bytes 1048608 | tf_op jit(solution)/shard_map/ppermute | solution.py:292
  19.2 1.6 %collective-permute-start.2 = (bf16[2048,128]{1,0:T(8,128)(2,1)S(1)}, bf16[2048,128]{1,0:T(8,128)(2,1)S(1)}, u32[]{:S(2)}, u32[]{:S(2)}) collective-permute-start(bf16[2048,128]{1,0:T(8,128)(2,1)S(1)} %get-tuple-element.57), channel_id=1, source_target_pairs={{0,16},{4,12},{8,24},{12,4},{16,0},{20,28},{24,8},{28,20},{1,17},{... | collective-permute-start | bytes 1572872 | tf_op jit(solution)/shard_map/ppermute | solution.py:292
  20.9 6.2 %collective-permute-done.1.refs_3_ = bf16[4096,128]{1,0:T(8,128)(2,1)S(1)} collective-permute-done((bf16[4096,128]{1,0:T(8,128)(2,1)S(1)}, bf16[4096,128]{1,0:T(8,128)(2,1)S(1)}, u32[]{:S(2)}, u32[]{:S(2)}) %collective-permute-start.1) | collective-permute-done | bytes 1048608 | tf_op jit(solution)/shard_map/ppermute | solution.py:292
  27.1 1.7 %collective-permute-start.6 = (bf16[2048,128]{1,0:T(8,128)(2,1)S(1)}, bf16[2048,128]{1,0:T(8,128)(2,1)S(1)}, u32[]{:S(2)}, u32[]{:S(2)}) collective-permute-start(bf16[2048,128]{1,0:T(8,128)(2,1)S(1)} %get-tuple-element.56), channel_id=1, source_target_pairs={{0,16},{4,12},{8,24},{12,4},{16,0},{20,28},{24,8},{28,20},{1,17},{... | collective-permute-start | bytes 1572872 | tf_op jit(solution)/shard_map/ppermute | solution.py:292
  28.8 4.3 %score_3_False.1 = (f32[16,2,256,256]{3,2,1,0:T(8,128)S(1)}, f32[8,128]{1,0:T(8,128)}) custom-call(s32[2,16]{1,0:T(2,128)S(1)} %bitcast.18, s32[1,16]{1,0:T(1,128)S(1)} %bitcast.21, bf16[4096,1024]{1,0:T(8,128)(2,1)S(1)} %copy-done.1, bf16[4096,128]{1,0:T(8,128)(2,1)S(1)} %collective-permute-done.3.refs_3_, ...), custom_call_target="tpu_custom_call" | custom-call | flops 8192 | bytes 1024 | tf_op jit(solution)/shard_map/score_3_False/pallas_call | solution.py:36
  34.0 4.3 %collective-permute-done.6 = bf16[2048,128]{1,0:T(8,128)(2,1)S(1)} collective-permute-done((bf16[2048,128]{1,0:T(8,128)(2,1)S(1)}, bf16[2048,128]{1,0:T(8,128)(2,1)S(1)}, u32[]{:S(2)}, u32[]{:S(2)}) %collective-permute-start.6) | collective-permute-done | bytes 524320 | tf_op jit(solution)/shard_map/ppermute | solution.py:292
  39.0 1.5 %collective-permute-done.8 = bf16[2048,128]{1,0:T(8,128)(2,1)S(1)} collective-permute-done((bf16[2048,128]{1,0:T(8,128)(2,1)S(1)}, bf16[2048,128]{1,0:T(8,128)(2,1)S(1)}, u32[]{:S(2)}, u32[]{:S(2)}) %collective-permute-start.8) | collective-permute-done | bytes 524320 | tf_op jit(solution)/shard_map/ppermute | solution.py:292
  40.6 4.2 %score_4_True.1 = (f32[16,2,256,256]{3,2,1,0:T(8,128)S(1)}, f32[2,16,256]{2,1,0:T(8,128)S(1)}) custom-call(s32[2,16]{1,0:T(2,128)S(1)} %bitcast.19, s32[1,16]{1,0:T(1,128)S(1)} %bitcast.22, bf16[4096,1024]{1,0:T(8,128)(2,1)S(1)} %copy-done.1, bf16[4096,128]{1,0:T(8,128)(2,1)S(1)} %collective-permute-done.1.refs_3_, ...), custom_call_target="tpu_custom_call" | custom-call | flops 8192 | bytes 1024 | tf_op jit(solution)/shard_map/score_4_True/pallas_call | solution.py:36
  44.7 4.2 %collective-permute-start.10 = (f32[2,16,256]{2,1,0:T(8,128)S(1)}, f32[2,16,256]{2,1,0:T(8,128)S(1)}, u32[]{:S(2)}, u32[]{:S(2)}) collective-permute-start(f32[2,16,256]{2,1,0:T(8,128)S(1)} %get-tuple-element.45.stats.refs_0_), channel_id=1, source_target_pairs={{0,3},{1,2},{2,1},{3,0},{4,5},{5,4},{6,7},{7,6},{8,11},{9,10},{10,... | collective-permute-start | bytes 98312 | tf_op jit(solution)/shard_map/ppermute | solution.py:326
  49.6 1.2 %exps.1.before = f32[16,2,256,256]{3,2,1,0:T(8,128)S(1)} custom-call(f32[16,2,256,256]{3,2,1,0:T(8,128)S(1)} %get-tuple-element.44.score, f32[2,16,256]{2,1,0:T(8,128)S(1)} %get-tuple-element.45.stats.refs_0_), custom_call_target="tpu_custom_call" | custom-call | flops 8192 | bytes 1024 | tf_op jit(solution)/shard_map/exps/pallas_call | solution.py:36
  51.1 2.6 %collective-permute-done.11.refs_3_ = f32[2,16,256]{2,1,0:T(8,128)S(1)} collective-permute-done((f32[2,16,256]{2,1,0:T(8,128)S(1)}, f32[2,16,256]{2,1,0:T(8,128)S(1)}, u32[]{:S(2)}, u32[]{:S(2)}) %collective-permute-start.11) | collective-permute-done | bytes 32800 | tf_op jit(solution)/shard_map/ppermute | solution.py:326
  53.8 1.3 %column_0.1 = (f32[16,2,256,256]{3,2,1,0:T(8,128)S(1)}, f32[2,16,256]{2,1,0:T(8,128)S(1)}, f32[32,256]{1,0:T(8,128)S(1)}, f32[16,256]{1,0:T(8,128)S(1)}, f32[16,256]{1,0:T(8,128)S(1)}) custom-call(f32[32,256]{1,0:T(8,128)S(1)} %get-tuple-element.32.names.refs_0_, f32[16,2,256,256]{3,2,1,0:T(8,128)S(1)} %get-tuple-element.44.score, ...), custom_call_target="tpu_custom_call", output_to_operand_aliasing={{0}: (2, {})} | custom-call | flops 8192 | bytes 1024 | tf_op jit(solution)/shard_map/column_0/pallas_call | solution.py:36
  55.2 1.2 %collective-permute-done.12 = f32[2,16,256]{2,1,0:T(8,128)S(1)} collective-permute-done((f32[2,16,256]{2,1,0:T(8,128)S(1)}, f32[2,16,256]{2,1,0:T(8,128)S(1)}, u32[]{:S(2)}, u32[]{:S(2)}) %collective-permute-start.12) | collective-permute-done | bytes 32800 | tf_op jit(solution)/shard_map/ppermute | solution.py:292
  56.5 2.4 %collective-permute-start.13 = (f32[2,16,256]{2,1,0:T(8,128)S(1)}, f32[2,16,256]{2,1,0:T(8,128)S(1)}, u32[]{:S(2)}, u32[]{:S(2)}) collective-permute-start(f32[2,16,256]{2,1,0:T(8,128)S(1)} %broadcast_select_fusion.refs_0_), channel_id=1, source_target_pairs={{0,24},{1,25},{2,26},{3,27},{4,12},{5,13},{6,14},{7,15},{8,16},{9,... | collective-permute-start | bytes 98312 | tf_op jit(solution)/shard_map/ppermute | solution.py:326
  60.0 1.4 %collective-permute-done.13.refs_1_ = f32[2,16,256]{2,1,0:T(8,128)S(1)} collective-permute-done((f32[2,16,256]{2,1,0:T(8,128)S(1)}, f32[2,16,256]{2,1,0:T(8,128)S(1)}, u32[]{:S(2)}, u32[]{:S(2)}) %collective-permute-start.13) | collective-permute-done | bytes 32800 | tf_op jit(solution)/shard_map/ppermute | solution.py:326
  61.4 1.5 %collective-permute-done.14.refs_2_ = f32[2,16,256]{2,1,0:T(8,128)S(1)} collective-permute-done((f32[2,16,256]{2,1,0:T(8,128)S(1)}, f32[2,16,256]{2,1,0:T(8,128)S(1)}, u32[]{:S(2)}, u32[]{:S(2)}) %collective-permute-start.14) | collective-permute-done | bytes 32800 | tf_op jit(solution)/shard_map/ppermute | solution.py:326
  64.1 1.6 %collective-permute-start.16 = (f32[16,256]{1,0:T(8,128)S(1)}, f32[16,256]{1,0:T(8,128)S(1)}, u32[]{:S(2)}, u32[]{:S(2)}) collective-permute-start(f32[16,256]{1,0:T(8,128)S(1)} %get-tuple-element.52.refs_5_), channel_id=1, source_target_pairs={{0,3},{1,2},{2,1},{3,0},{4,5},{5,4},{6,7},{7,6},{8,11},{9,10},{10,... | collective-permute-start | bytes 49160 | tf_op jit(solution)/shard_map/ppermute | solution.py:326
  66.2 2.3 %collective-permute-start.18 = (f32[16,256]{1,0:T(8,128)S(1)}, f32[16,256]{1,0:T(8,128)S(1)}, u32[]{:S(2)}, u32[]{:S(2)}) collective-permute-start(f32[16,256]{1,0:T(8,128)S(1)} %get-tuple-element.52.refs_5_), channel_id=1, source_target_pairs={{0,1},{1,0},{2,3},{3,2},{4,6},{5,7},{6,4},{7,5},{8,9},{9,8},{10,11... | collective-permute-start | bytes 49160 | tf_op jit(solution)/shard_map/ppermute | solution.py:326
  71.4 1.2 %collective-permute-done.19 = f32[16,256]{1,0:T(8,128)S(1)} collective-permute-done((f32[16,256]{1,0:T(8,128)S(1)}, f32[16,256]{1,0:T(8,128)S(1)}, u32[]{:S(2)}, u32[]{:S(2)}) %collective-permute-start.19) | collective-permute-done | bytes 16416 | tf_op jit(solution)/shard_map/ppermute | solution.py:292
  72.5 1.6 %collective-permute-start.20 = (f32[16,256]{1,0:T(8,128)S(1)}, f32[16,256]{1,0:T(8,128)S(1)}, u32[]{:S(2)}, u32[]{:S(2)}) collective-permute-start(f32[16,256]{1,0:T(8,128)S(1)} %add.11.refs_0_), channel_id=1, source_target_pairs={{0,24},{1,25},{2,26},{3,27},{4,12},{5,13},{6,14},{7,15},{8,16},{9,... | collective-permute-start | bytes 49160 | tf_op jit(solution)/shard_map/ppermute | solution.py:326
  74.8 1.2 %collective-permute-start.22 = (f32[16,256]{1,0:T(8,128)S(1)}, f32[16,256]{1,0:T(8,128)S(1)}, u32[]{:S(2)}, u32[]{:S(2)}) collective-permute-start(f32[16,256]{1,0:T(8,128)S(1)} %add.11.refs_0_), channel_id=1, source_target_pairs={{0,8},{1,9},{2,10},{3,11},{4,20},{5,21},{6,22},{7,23},{8,0},{9,1},... | collective-permute-start | bytes 49160 | tf_op jit(solution)/shard_map/ppermute | solution.py:326
  79.3 2.2 %collective-permute-start.23 = (f32[16,256]{1,0:T(8,128)S(1)}, f32[16,256]{1,0:T(8,128)S(1)}, u32[]{:S(2)}, u32[]{:S(2)}) collective-permute-start(f32[16,256]{1,0:T(8,128)S(1)} %row_2.1.refs_6_), channel_id=1, source_target_pairs={{0,3},{1,2},{2,1},{3,0},{4,5},{5,4},{6,7},{7,6},{8,11},{9,10},{10,... | collective-permute-start | bytes 49160 | tf_op jit(solution)/shard_map/ppermute | solution.py:326
  82.5 1.3 %collective-permute-start.25 = (f32[16,256]{1,0:T(8,128)S(1)}, f32[16,256]{1,0:T(8,128)S(1)}, u32[]{:S(2)}, u32[]{:S(2)}) collective-permute-start(f32[16,256]{1,0:T(8,128)S(1)} %row_2.1.refs_6_), channel_id=1, source_target_pairs={{0,1},{1,0},{2,3},{3,2},{4,6},{5,7},{6,4},{7,5},{8,9},{9,8},{10,11... | collective-permute-start | bytes 49160 | tf_op jit(solution)/shard_map/ppermute | solution.py:326
  83.8 1.3 %collective-permute-done.23.refs_7_ = f32[16,256]{1,0:T(8,128)S(1)} collective-permute-done((f32[16,256]{1,0:T(8,128)S(1)}, f32[16,256]{1,0:T(8,128)S(1)}, u32[]{:S(2)}, u32[]{:S(2)}) %collective-permute-start.23) | collective-permute-done | bytes 16416 | tf_op jit(solution)/shard_map/ppermute | solution.py:326
  87.3 1.2 %collective-permute-done.26 = f32[16,256]{1,0:T(8,128)S(1)} collective-permute-done((f32[16,256]{1,0:T(8,128)S(1)}, f32[16,256]{1,0:T(8,128)S(1)}, u32[]{:S(2)}, u32[]{:S(2)}) %collective-permute-start.26) | collective-permute-done | bytes 16416 | tf_op jit(solution)/shard_map/ppermute | solution.py:292
  88.5 2.4 %collective-permute-start.27 = (f32[16,256]{1,0:T(8,128)S(1)}, f32[16,256]{1,0:T(8,128)S(1)}, u32[]{:S(2)}, u32[]{:S(2)}) collective-permute-start(f32[16,256]{1,0:T(8,128)S(1)} %add.12.refs_0_), channel_id=1, source_target_pairs={{0,24},{1,25},{2,26},{3,27},{4,12},{5,13},{6,14},{7,15},{8,16},{9,... | collective-permute-start | bytes 49160 | tf_op jit(solution)/shard_map/ppermute | solution.py:326
  93.1 1.5 %collective-permute-done.28.refs_2_ = f32[16,256]{1,0:T(8,128)S(1)} collective-permute-done((f32[16,256]{1,0:T(8,128)S(1)}, f32[16,256]{1,0:T(8,128)S(1)}, u32[]{:S(2)}, u32[]{:S(2)}) %collective-permute-start.28) | collective-permute-done | bytes 16416 | tf_op jit(solution)/shard_map/ppermute | solution.py:326
  (65 shorter events, 20.2 us)
Async XLA Ops:
  0.6 28.2 %copy-start.6 = (s32[16,2]{0,1:T(2,128)S(1)}, s32[16,2]{0,1:T(2,128)}, u32[]{:S(2)}) copy-start(s32[16,2]{0,1:T(2,128)} %param.10) | copy-start | bytes 388
  0.6 28.2 %copy-start.8 = (s32[16,1]{0,1:T(1,128)S(1)}, s32[16,1]{0,1:T(1,128)}, u32[]{:S(2)}) copy-start(s32[16,1]{0,1:T(1,128)} %param.11) | copy-start | bytes 196
  0.7 18.5 %collective-permute-start = (bf16[4096,128]{1,0:T(8,128)(2,1)}, bf16[4096,128]{1,0:T(8,128)(2,1)S(1)}, u32[]{:S(2)}, u32[]{:S(2)}) collective-permute-start(bf16[4096,128]{1,0:T(8,128)(2,1)} %refs_3_.1), channel_id=1, source_target_pairs={{0,8},{4,20},{8,0},{12,28},{16,24},{20,4},{24,16},{28,12},{1,9},{5... | collective-permute-start | bytes 3145736 | tf_op jit(solution)/shard_map/ppermute | solution.py:292
  3.7 25.1 %collective-permute-start.3 = (bf16[4096,128]{1,0:T(8,128)(2,1)}, bf16[4096,128]{1,0:T(8,128)(2,1)S(1)}, u32[]{:S(2)}, u32[]{:S(2)}) collective-permute-start(bf16[4096,128]{1,0:T(8,128)(2,1)} %refs_3_.1), channel_id=1, source_target_pairs={{0,4},{4,0},{8,12},{12,8},{16,20},{20,16},{24,28},{28,24},{1,5},{5... | collective-permute-start | bytes 3145736 | tf_op jit(solution)/shard_map/ppermute | solution.py:292
  12.0 15.1 %collective-permute-start.1 = (bf16[4096,128]{1,0:T(8,128)(2,1)S(1)}, bf16[4096,128]{1,0:T(8,128)(2,1)S(1)}, u32[]{:S(2)}, u32[]{:S(2)}) collective-permute-start(bf16[4096,128]{1,0:T(8,128)(2,1)S(1)} %copy-done.2), channel_id=1, source_target_pairs={{0,16},{4,12},{8,24},{12,4},{16,0},{20,28},{24,8},{28,20},{1,17},{... | collective-permute-start | bytes 3145736 | tf_op jit(solution)/shard_map/ppermute | solution.py:292
  19.2 9.6 %collective-permute-start.4 = (bf16[4096,128]{1,0:T(8,128)(2,1)S(1)}, bf16[4096,128]{1,0:T(8,128)(2,1)S(1)}, u32[]{:S(2)}, u32[]{:S(2)}) collective-permute-start(bf16[4096,128]{1,0:T(8,128)(2,1)S(1)} %collective-permute-done.refs_4_), channel_id=1, source_target_pairs={{0,4},{4,0},{8,12},{12,8},{16,20},{20,16},{24,28},{28,24},{1,5},{5... | collective-permute-start | bytes 3145736 | tf_op jit(solution)/shard_map/ppermute | solution.py:292
  19.2 13.8 %collective-permute-start.2 = (bf16[2048,128]{1,0:T(8,128)(2,1)S(1)}, bf16[2048,128]{1,0:T(8,128)(2,1)S(1)}, u32[]{:S(2)}, u32[]{:S(2)}) collective-permute-start(bf16[2048,128]{1,0:T(8,128)(2,1)S(1)} %get-tuple-element.57), channel_id=1, source_target_pairs={{0,16},{4,12},{8,24},{12,4},{16,0},{20,28},{24,8},{28,20},{1,17},{... | collective-permute-start | bytes 1572872 | tf_op jit(solution)/shard_map/ppermute | solution.py:292
  27.1 11.2 %collective-permute-start.6 = (bf16[2048,128]{1,0:T(8,128)(2,1)S(1)}, bf16[2048,128]{1,0:T(8,128)(2,1)S(1)}, u32[]{:S(2)}, u32[]{:S(2)}) collective-permute-start(bf16[2048,128]{1,0:T(8,128)(2,1)S(1)} %get-tuple-element.56), channel_id=1, source_target_pairs={{0,16},{4,12},{8,24},{12,4},{16,0},{20,28},{24,8},{28,20},{1,17},{... | collective-permute-start | bytes 1572872 | tf_op jit(solution)/shard_map/ppermute | solution.py:292
  33.1 5.2 %collective-permute-start.7 = (bf16[2048,128]{1,0:T(8,128)(2,1)S(1)}, bf16[2048,128]{1,0:T(8,128)(2,1)S(1)}, u32[]{:S(2)}, u32[]{:S(2)}) collective-permute-start(bf16[2048,128]{1,0:T(8,128)(2,1)S(1)} %collective-permute-done.2), channel_id=1, source_target_pairs={{0,4},{4,0},{8,12},{12,8},{16,20},{20,16},{24,28},{28,24},{1,5},{5... | collective-permute-start | bytes 1572872 | tf_op jit(solution)/shard_map/ppermute | solution.py:292
  34.0 6.5 %collective-permute-start.5 = (bf16[4096,128]{1,0:T(8,128)(2,1)S(1)}, bf16[4096,128]{1,0:T(8,128)(2,1)S(1)}, u32[]{:S(2)}, u32[]{:S(2)}) collective-permute-start(bf16[4096,128]{1,0:T(8,128)(2,1)S(1)} %collective-permute-done.1.refs_3_), channel_id=1, source_target_pairs={{0,4},{4,0},{8,12},{12,8},{16,20},{20,16},{24,28},{28,24},{1,5},{5... | collective-permute-start | bytes 3145736 | tf_op jit(solution)/shard_map/ppermute | solution.py:292
  38.3 2.2 %collective-permute-start.8 = (bf16[2048,128]{1,0:T(8,128)(2,1)S(1)}, bf16[2048,128]{1,0:T(8,128)(2,1)S(1)}, u32[]{:S(2)}, u32[]{:S(2)}) collective-permute-start(bf16[2048,128]{1,0:T(8,128)(2,1)S(1)} %collective-permute-done.6), channel_id=1, source_target_pairs={{0,4},{4,0},{8,12},{12,8},{16,20},{20,16},{24,28},{28,24},{1,5},{5... | collective-permute-start | bytes 1572872 | tf_op jit(solution)/shard_map/ppermute | solution.py:292
  44.7 6.4 %collective-permute-start.10 = (f32[2,16,256]{2,1,0:T(8,128)S(1)}, f32[2,16,256]{2,1,0:T(8,128)S(1)}, u32[]{:S(2)}, u32[]{:S(2)}) collective-permute-start(f32[2,16,256]{2,1,0:T(8,128)S(1)} %get-tuple-element.45.stats.refs_0_), channel_id=1, source_target_pairs={{0,3},{1,2},{2,1},{3,0},{4,5},{5,4},{6,7},{7,6},{8,11},{9,10},{10,... | collective-permute-start | bytes 98312 | tf_op jit(solution)/shard_map/ppermute | solution.py:326
  48.9 4.8 %collective-permute-start.11 = (f32[2,16,256]{2,1,0:T(8,128)S(1)}, f32[2,16,256]{2,1,0:T(8,128)S(1)}, u32[]{:S(2)}, u32[]{:S(2)}) collective-permute-start(f32[2,16,256]{2,1,0:T(8,128)S(1)} %get-tuple-element.45.stats.refs_0_), channel_id=1, source_target_pairs={{0,2},{1,3},{2,0},{3,1},{4,7},{5,6},{6,5},{7,4},{8,10},{9,11},{10,... | collective-permute-start | bytes 98312 | tf_op jit(solution)/shard_map/ppermute | solution.py:326
  48.9 4.8 %collective-permute-start.9 = (f32[2,16,256]{2,1,0:T(8,128)S(1)}, f32[2,16,256]{2,1,0:T(8,128)S(1)}, u32[]{:S(2)}, u32[]{:S(2)}) collective-permute-start(f32[2,16,256]{2,1,0:T(8,128)S(1)} %get-tuple-element.45.stats.refs_0_), channel_id=1, source_target_pairs={{0,1},{1,0},{2,3},{3,2},{4,6},{5,7},{6,4},{7,5},{8,9},{9,8},{10,11... | collective-permute-start | bytes 98312 | tf_op jit(solution)/shard_map/ppermute | solution.py:326
  55.2 1.3 %collective-permute-start.12 = (f32[2,16,256]{2,1,0:T(8,128)S(1)}, f32[2,16,256]{2,1,0:T(8,128)S(1)}, u32[]{:S(2)}, u32[]{:S(2)}) collective-permute-start(f32[2,16,256]{2,1,0:T(8,128)S(1)} %get-tuple-element.49), channel_id=1, source_target_pairs={{0,4},{4,0},{8,12},{12,8},{16,20},{20,16},{24,28},{28,24},{1,5},{5... | collective-permute-start | bytes 98312 | tf_op jit(solution)/shard_map/ppermute | solution.py:292
  56.5 4.9 %collective-permute-start.13 = (f32[2,16,256]{2,1,0:T(8,128)S(1)}, f32[2,16,256]{2,1,0:T(8,128)S(1)}, u32[]{:S(2)}, u32[]{:S(2)}) collective-permute-start(f32[2,16,256]{2,1,0:T(8,128)S(1)} %broadcast_select_fusion.refs_0_), channel_id=1, source_target_pairs={{0,24},{1,25},{2,26},{3,27},{4,12},{5,13},{6,14},{7,15},{8,16},{9,... | collective-permute-start | bytes 98312 | tf_op jit(solution)/shard_map/ppermute | solution.py:326
  59.0 3.9 %collective-permute-start.14 = (f32[2,16,256]{2,1,0:T(8,128)S(1)}, f32[2,16,256]{2,1,0:T(8,128)S(1)}, u32[]{:S(2)}, u32[]{:S(2)}) collective-permute-start(f32[2,16,256]{2,1,0:T(8,128)S(1)} %broadcast_select_fusion.refs_0_), channel_id=1, source_target_pairs={{0,16},{1,17},{2,18},{3,19},{4,28},{5,29},{6,30},{7,31},{8,24},{9,... | collective-permute-start | bytes 98312 | tf_op jit(solution)/shard_map/ppermute | solution.py:326
  59.4 3.9 %collective-permute-start.15 = (f32[2,16,256]{2,1,0:T(8,128)S(1)}, f32[2,16,256]{2,1,0:T(8,128)S(1)}, u32[]{:S(2)}, u32[]{:S(2)}) collective-permute-start(f32[2,16,256]{2,1,0:T(8,128)S(1)} %broadcast_select_fusion.refs_0_), channel_id=1, source_target_pairs={{0,8},{1,9},{2,10},{3,11},{4,20},{5,21},{6,22},{7,23},{8,0},{9,1},... | collective-permute-start | bytes 98312 | tf_op jit(solution)/shard_map/ppermute | solution.py:326
  64.1 5.6 %collective-permute-start.16 = (f32[16,256]{1,0:T(8,128)S(1)}, f32[16,256]{1,0:T(8,128)S(1)}, u32[]{:S(2)}, u32[]{:S(2)}) collective-permute-start(f32[16,256]{1,0:T(8,128)S(1)} %get-tuple-element.52.refs_5_), channel_id=1, source_target_pairs={{0,3},{1,2},{2,1},{3,0},{4,5},{5,4},{6,7},{7,6},{8,11},{9,10},{10,... | collective-permute-start | bytes 49160 | tf_op jit(solution)/shard_map/ppermute | solution.py:326
  65.7 4.7 %collective-permute-start.17 = (f32[16,256]{1,0:T(8,128)S(1)}, f32[16,256]{1,0:T(8,128)S(1)}, u32[]{:S(2)}, u32[]{:S(2)}) collective-permute-start(f32[16,256]{1,0:T(8,128)S(1)} %get-tuple-element.52.refs_5_), channel_id=1, source_target_pairs={{0,2},{1,3},{2,0},{3,1},{4,7},{5,6},{6,5},{7,4},{8,10},{9,11},{10,... | collective-permute-start | bytes 49160 | tf_op jit(solution)/shard_map/ppermute | solution.py:326
  66.2 4.2 %collective-permute-start.18 = (f32[16,256]{1,0:T(8,128)S(1)}, f32[16,256]{1,0:T(8,128)S(1)}, u32[]{:S(2)}, u32[]{:S(2)}) collective-permute-start(f32[16,256]{1,0:T(8,128)S(1)} %get-tuple-element.52.refs_5_), channel_id=1, source_target_pairs={{0,1},{1,0},{2,3},{3,2},{4,6},{5,7},{6,4},{7,5},{8,9},{9,8},{10,11... | collective-permute-start | bytes 49160 | tf_op jit(solution)/shard_map/ppermute | solution.py:326
  71.3 1.2 %collective-permute-start.19 = (f32[16,256]{1,0:T(8,128)S(1)}, f32[16,256]{1,0:T(8,128)S(1)}, u32[]{:S(2)}, u32[]{:S(2)}) collective-permute-start(f32[16,256]{1,0:T(8,128)S(1)} %column_1.1), channel_id=1, source_target_pairs={{0,4},{4,0},{8,12},{12,8},{16,20},{20,16},{24,28},{28,24},{1,5},{5... | collective-permute-start | bytes 49160 | tf_op jit(solution)/shard_map/ppermute | solution.py:292
  72.5 4.6 %collective-permute-start.20 = (f32[16,256]{1,0:T(8,128)S(1)}, f32[16,256]{1,0:T(8,128)S(1)}, u32[]{:S(2)}, u32[]{:S(2)}) collective-permute-start(f32[16,256]{1,0:T(8,128)S(1)} %add.11.refs_0_), channel_id=1, source_target_pairs={{0,24},{1,25},{2,26},{3,27},{4,12},{5,13},{6,14},{7,15},{8,16},{9,... | collective-permute-start | bytes 49160 | tf_op jit(solution)/shard_map/ppermute | solution.py:326
  74.2 3.8 %collective-permute-start.21 = (f32[16,256]{1,0:T(8,128)S(1)}, f32[16,256]{1,0:T(8,128)S(1)}, u32[]{:S(2)}, u32[]{:S(2)}) collective-permute-start(f32[16,256]{1,0:T(8,128)S(1)} %add.11.refs_0_), channel_id=1, source_target_pairs={{0,16},{1,17},{2,18},{3,19},{4,28},{5,29},{6,30},{7,31},{8,24},{9,... | collective-permute-start | bytes 49160 | tf_op jit(solution)/shard_map/ppermute | solution.py:326
  74.8 3.7 %collective-permute-start.22 = (f32[16,256]{1,0:T(8,128)S(1)}, f32[16,256]{1,0:T(8,128)S(1)}, u32[]{:S(2)}, u32[]{:S(2)}) collective-permute-start(f32[16,256]{1,0:T(8,128)S(1)} %add.11.refs_0_), channel_id=1, source_target_pairs={{0,8},{1,9},{2,10},{3,11},{4,20},{5,21},{6,22},{7,23},{8,0},{9,1},... | collective-permute-start | bytes 49160 | tf_op jit(solution)/shard_map/ppermute | solution.py:326
  79.3 5.8 %collective-permute-start.23 = (f32[16,256]{1,0:T(8,128)S(1)}, f32[16,256]{1,0:T(8,128)S(1)}, u32[]{:S(2)}, u32[]{:S(2)}) collective-permute-start(f32[16,256]{1,0:T(8,128)S(1)} %row_2.1.refs_6_), channel_id=1, source_target_pairs={{0,3},{1,2},{2,1},{3,0},{4,5},{5,4},{6,7},{7,6},{8,11},{9,10},{10,... | collective-permute-start | bytes 49160 | tf_op jit(solution)/shard_map/ppermute | solution.py:326
  81.6 4.6 %collective-permute-start.24 = (f32[16,256]{1,0:T(8,128)S(1)}, f32[16,256]{1,0:T(8,128)S(1)}, u32[]{:S(2)}, u32[]{:S(2)}) collective-permute-start(f32[16,256]{1,0:T(8,128)S(1)} %row_2.1.refs_6_), channel_id=1, source_target_pairs={{0,2},{1,3},{2,0},{3,1},{4,7},{5,6},{6,5},{7,4},{8,10},{9,11},{10,... | collective-permute-start | bytes 49160 | tf_op jit(solution)/shard_map/ppermute | solution.py:326
  82.5 3.9 %collective-permute-start.25 = (f32[16,256]{1,0:T(8,128)S(1)}, f32[16,256]{1,0:T(8,128)S(1)}, u32[]{:S(2)}, u32[]{:S(2)}) collective-permute-start(f32[16,256]{1,0:T(8,128)S(1)} %row_2.1.refs_6_), channel_id=1, source_target_pairs={{0,1},{1,0},{2,3},{3,2},{4,6},{5,7},{6,4},{7,5},{8,9},{9,8},{10,11... | collective-permute-start | bytes 49160 | tf_op jit(solution)/shard_map/ppermute | solution.py:326
  87.2 1.2 %collective-permute-start.26 = (f32[16,256]{1,0:T(8,128)S(1)}, f32[16,256]{1,0:T(8,128)S(1)}, u32[]{:S(2)}, u32[]{:S(2)}) collective-permute-start(f32[16,256]{1,0:T(8,128)S(1)} %get-tuple-element.55), channel_id=1, source_target_pairs={{0,4},{4,0},{8,12},{12,8},{16,20},{20,16},{24,28},{28,24},{1,5},{5... | collective-permute-start | bytes 49160 | tf_op jit(solution)/shard_map/ppermute | solution.py:292
  88.5 4.6 %collective-permute-start.27 = (f32[16,256]{1,0:T(8,128)S(1)}, f32[16,256]{1,0:T(8,128)S(1)}, u32[]{:S(2)}, u32[]{:S(2)}) collective-permute-start(f32[16,256]{1,0:T(8,128)S(1)} %add.12.refs_0_), channel_id=1, source_target_pairs={{0,24},{1,25},{2,26},{3,27},{4,12},{5,13},{6,14},{7,15},{8,16},{9,... | collective-permute-start | bytes 49160 | tf_op jit(solution)/shard_map/ppermute | solution.py:326
  90.9 3.7 %collective-permute-start.28 = (f32[16,256]{1,0:T(8,128)S(1)}, f32[16,256]{1,0:T(8,128)S(1)}, u32[]{:S(2)}, u32[]{:S(2)}) collective-permute-start(f32[16,256]{1,0:T(8,128)S(1)} %add.12.refs_0_), channel_id=1, source_target_pairs={{0,16},{1,17},{2,18},{3,19},{4,28},{5,29},{6,30},{7,31},{8,24},{9,... | collective-permute-start | bytes 49160 | tf_op jit(solution)/shard_map/ppermute | solution.py:326
  91.3 3.7 %collective-permute-start.29 = (f32[16,256]{1,0:T(8,128)S(1)}, f32[16,256]{1,0:T(8,128)S(1)}, u32[]{:S(2)}, u32[]{:S(2)}) collective-permute-start(f32[16,256]{1,0:T(8,128)S(1)} %add.12.refs_0_), channel_id=1, source_target_pairs={{0,8},{1,9},{2,10},{3,11},{4,20},{5,21},{6,22},{7,23},{8,0},{9,1},... | collective-permute-start | bytes 49160 | tf_op jit(solution)/shard_map/ppermute | solution.py:326
  (7 other events, 38.9 us)

commit v2 on v1

--- a/solution.py
+++ b/solution.py
@@ -11,6 +11,7 @@
 TILE = 256
 LANES = 128
 STRIP = 32
+FINE = 16
 HALF = 64
 LOW = -1e30
 FLOOR = -1e29
@@ -59,8 +60,9 @@
 
 
 def put_lanes(ref, start, columns):
-    rows = pl.ds(start, STRIP)
-    lane = lax.broadcasted_iota(jnp.int32, (STRIP, LANES), 1)
+    size = next(iter(columns.values())).shape[0]
+    rows = pl.ds(start, size)
+    lane = lax.broadcasted_iota(jnp.int32, (size, LANES), 1)
     value = ref[rows, :]
     for at, column in columns.items():
         value = jnp.where(lane == at, column, value)
@@ -122,8 +124,8 @@
             score[t, s] = block
 
     def statistics(t):
-        for r in range(0, TILE, STRIP):
-            blocks = [score[t, s, r : r + STRIP] for s in range(slots)]
+        for r in range(0, TILE, FINE):
+            blocks = [score[t, s, r : r + FINE] for s in range(slots)]
             top = halves(functools.reduce(jnp.maximum, blocks), jnp.maximum)
             top = jnp.max(top, axis=1, keepdims=True)
             total = functools.reduce(jnp.add, [jnp.exp2(block - top) for block in blocks])
@@ -208,8 +210,11 @@
     factor[...] = jnp.exp2(gathered[0][0] + row)
     columns[...] = to_columns(factor[...])
     slot_sums(before, columns, sums)
+    named = names[...]
     tops[...] = jnp.zeros(tops.shape, jnp.float32)
-    least = jnp.min(jnp.where(names[...] >= 0, sums[...], 1.0))
+    to_targets(named, sums[...], stats.at[1], jnp.sum, 0.0)
+    stats[0] = jnp.where(stats[1] > 0.0, 0.0, FLOOR)
+    least = jnp.min(jnp.where(named >= 0, sums[...], 1.0))
 
     @pl.when(least < LEAST)
     def _():
@@ -234,11 +239,9 @@
                 k = t * slots + s
                 tops[k : k + 1, :] = best[s]
                 sums[k : k + 1, :] = jnp.sum(total[s], axis=0, keepdims=True)
-
-    named = names[...]
-    to_targets(named, tops[...], stats.at[0], jnp.max, FLOOR)
-    change = jnp.exp2(tops[...] - to_slots(named, stats[0]))
-    to_targets(named, sums[...] * change, stats.at[1], jnp.sum, 0.0)
+        to_targets(named, tops[...], stats.at[0], jnp.max, FLOOR)
+        change = jnp.exp2(tops[...] - to_slots(named, stats[0]))
+        to_targets(named, sums[...] * change, stats.at[1], jnp.sum, 0.0)
 
 
 def row_sums(kernel, weights, factor, out, columns):
@@ -341,8 +344,8 @@
     later, names = lax.optimization_barrier((target, names))
     second = permute(later, "row", n, second_way)
     first, part, names = lax.optimization_barrier((first, part, names))
-    half = first.shape[0] // 2
-    early, late = (permute(part, "row", n, second_way) for part in (first[:half], first[half:]))
+    cut = first.shape[0] // 2
+    early, late = (permute(part, "row", n, second_way) for part in (first[:cut], first[cut:]))
     sibling = swap(target, "row", n, 1)
     first_sibling = swap(first, "row", n, 1)
     part, second = lax.optimization_barrier((part, second))

time: 95.9 us -> 95.8 us (level)
  no operation moved by 1% of the time
where the time goes in v2:
time: 95.8 us; the launch traced here: 95.6 us
  waiting for transfers between devices  36.8 us (38%)
  starting transfers between devices  34 us (35%)
  Pallas kernels  17.1 us (18%)
  local copies, waits for them, and re-layouts  6.63 us (7%)
    ppermute x18, starting transfers between devices, exchange(): parts.append(lax.ppermute(x, ('row', 'col'), pairs))  24.2 us
    ppermute x12, waiting for transfers between devices, permute(): return lax.ppermute(x, axis, [(i, partner(i)) for i in range(n)])  21.1 us
    pallas_call x10, Pallas kernels, kernel_call(): pl.pallas_call(body, out_shape=[(jax.ShapeDtypeStruct if final else VMEM)...  17.1 us
    ppermute x18, waiting for transfers between devices, exchange(): parts.append(lax.ppermute(x, ('row', 'col'), pairs))  15.7 us
    ppermute x12, starting transfers between devices, permute(): return lax.ppermute(x, axis, [(i, partner(i)) for i in range(n)])  9.77 us
    unnamed x19, local copies, waits for them, and re-layouts  6.56 us
  transfers between devices with their start and end apart: 30, of which 23 were waited for; matrix products, arithmetic and copies ran while one was open for 1% of the time, Pallas kernels for 8%

profile of v2, /device:TPU:0, one launch (start us, length us, event | category | flops | bytes accessed | tf_op | source)
XLA Modules:
  0.0 95.6 jit_solution(4091074382927273086)
XLA Ops:
  0.7 3.0 %collective-permute-start = (bf16[4096,128]{1,0:T(8,128)(2,1)}, bf16[4096,128]{1,0:T(8,128)(2,1)S(1)}, u32[]{:S(2)}, u32[]{:S(2)}) collective-permute-start(bf16[4096,128]{1,0:T(8,128)(2,1)} %refs_3_.1), channel_id=1, source_target_pairs={{0,8},{4,20},{8,0},{12,28},{16,24},{20,4},{24,16},{28,12},{1,9},{5... | collective-permute-start | bytes 3145736 | tf_op jit(solution)/shard_map/ppermute | solution.py:295
  3.7 3.4 %copy-done = bf16[4096,1024]{1,0:T(8,128)(2,1)S(1)} copy-done((bf16[4096,1024]{1,0:T(8,128)(2,1)S(1)}, bf16[4096,1024]{1,0:T(8,128)(2,1)}, u32[]{:S(2)}) %copy-start) | copy-done | bytes 8388632
  7.0 1.2 %copy-done.2 = bf16[4096,128]{1,0:T(8,128)(2,1)S(1)} copy-done((bf16[4096,128]{1,0:T(8,128)(2,1)S(1)}, bf16[4096,128]{1,0:T(8,128)(2,1)}, u32[]{:S(2)}) %copy-start.2) | copy-done | bytes 1048600
  9.6 2.4 %score_1_False.1 = (f32[16,2,256,256]{3,2,1,0:T(8,128)S(1)}, f32[32,256]{1,0:T(8,128)S(1)}) custom-call(s32[2,16]{1,0:T(2,128)S(1)} %bitcast.17, s32[1,16]{1,0:T(1,128)S(1)} %bitcast.20, bf16[4096,1024]{1,0:T(8,128)(2,1)S(1)} %copy-done, bf16[4096,128]{1,0:T(8,128)(2,1)S(1)} %copy-done.2), custom_call_target="tpu_custom_call" | custom-call | flops 8192 | bytes 1024 | tf_op jit(solution)/shard_map/score_1_False/pallas_call | solution.py:37
  12.0 1.6 %collective-permute-start.1 = (bf16[4096,128]{1,0:T(8,128)(2,1)S(1)}, bf16[4096,128]{1,0:T(8,128)(2,1)S(1)}, u32[]{:S(2)}, u32[]{:S(2)}) collective-permute-start(bf16[4096,128]{1,0:T(8,128)(2,1)S(1)} %copy-done.2), channel_id=1, source_target_pairs={{0,16},{4,12},{8,24},{12,4},{16,0},{20,28},{24,8},{28,20},{1,17},{... | collective-permute-start | bytes 3145736 | tf_op jit(solution)/shard_map/ppermute | solution.py:295
  13.6 5.6 %collective-permute-done.refs_4_ = bf16[4096,128]{1,0:T(8,128)(2,1)S(1)} collective-permute-done((bf16[4096,128]{1,0:T(8,128)(2,1)}, bf16[4096,128]{1,0:T(8,128)(2,1)S(1)}, u32[]{:S(2)}, u32[]{:S(2)}) %collective-permute-start) | collective-permute-done | bytes 1048608 | tf_op jit(solution)/shard_map/ppermute | solution.py:295
  19.2 1.6 %collective-permute-start.2 = (bf16[2048,128]{1,0:T(8,128)(2,1)S(1)}, bf16[2048,128]{1,0:T(8,128)(2,1)S(1)}, u32[]{:S(2)}, u32[]{:S(2)}) collective-permute-start(bf16[2048,128]{1,0:T(8,128)(2,1)S(1)} %get-tuple-element.57), channel_id=1, source_target_pairs={{0,16},{4,12},{8,24},{12,4},{16,0},{20,28},{24,8},{28,20},{1,17},{... | collective-permute-start | bytes 1572872 | tf_op jit(solution)/shard_map/ppermute | solution.py:295
  20.9 6.2 %collective-permute-done.1.refs_3_ = bf16[4096,128]{1,0:T(8,128)(2,1)S(1)} collective-permute-done((bf16[4096,128]{1,0:T(8,128)(2,1)S(1)}, bf16[4096,128]{1,0:T(8,128)(2,1)S(1)}, u32[]{:S(2)}, u32[]{:S(2)}) %collective-permute-start.1) | collective-permute-done | bytes 1048608 | tf_op jit(solution)/shard_map/ppermute | solution.py:295
  27.1 1.7 %collective-permute-start.6 = (bf16[2048,128]{1,0:T(8,128)(2,1)S(1)}, bf16[2048,128]{1,0:T(8,128)(2,1)S(1)}, u32[]{:S(2)}, u32[]{:S(2)}) collective-permute-start(bf16[2048,128]{1,0:T(8,128)(2,1)S(1)} %get-tuple-element.56), channel_id=1, source_target_pairs={{0,16},{4,12},{8,24},{12,4},{16,0},{20,28},{24,8},{28,20},{1,17},{... | collective-permute-start | bytes 1572872 | tf_op jit(solution)/shard_map/ppermute | solution.py:295
  28.8 4.3 %score_3_False.1 = (f32[16,2,256,256]{3,2,1,0:T(8,128)S(1)}, f32[8,128]{1,0:T(8,128)}) custom-call(s32[2,16]{1,0:T(2,128)S(1)} %bitcast.18, s32[1,16]{1,0:T(1,128)S(1)} %bitcast.21, bf16[4096,1024]{1,0:T(8,128)(2,1)S(1)} %copy-done.1, bf16[4096,128]{1,0:T(8,128)(2,1)S(1)} %collective-permute-done.3.refs_3_, ...), custom_call_target="tpu_custom_call" | custom-call | flops 8192 | bytes 1024 | tf_op jit(solution)/shard_map/score_3_False/pallas_call | solution.py:37
  34.0 4.3 %collective-permute-done.6 = bf16[2048,128]{1,0:T(8,128)(2,1)S(1)} collective-permute-done((bf16[2048,128]{1,0:T(8,128)(2,1)S(1)}, bf16[2048,128]{1,0:T(8,128)(2,1)S(1)}, u32[]{:S(2)}, u32[]{:S(2)}) %collective-permute-start.6) | collective-permute-done | bytes 524320 | tf_op jit(solution)/shard_map/ppermute | solution.py:295
  39.0 1.5 %collective-permute-done.8 = bf16[2048,128]{1,0:T(8,128)(2,1)S(1)} collective-permute-done((bf16[2048,128]{1,0:T(8,128)(2,1)S(1)}, bf16[2048,128]{1,0:T(8,128)(2,1)S(1)}, u32[]{:S(2)}, u32[]{:S(2)}) %collective-permute-start.8) | collective-permute-done | bytes 524320 | tf_op jit(solution)/shard_map/ppermute | solution.py:295
  40.6 4.2 %score_4_True.1 = (f32[16,2,256,256]{3,2,1,0:T(8,128)S(1)}, f32[2,16,256]{2,1,0:T(8,128)S(1)}) custom-call(s32[2,16]{1,0:T(2,128)S(1)} %bitcast.19, s32[1,16]{1,0:T(1,128)S(1)} %bitcast.22, bf16[4096,1024]{1,0:T(8,128)(2,1)S(1)} %copy-done.1, bf16[4096,128]{1,0:T(8,128)(2,1)S(1)} %collective-permute-done.1.refs_3_, ...), custom_call_target="tpu_custom_call" | custom-call | flops 8192 | bytes 1024 | tf_op jit(solution)/shard_map/score_4_True/pallas_call | solution.py:37
  44.7 4.2 %collective-permute-start.10 = (f32[2,16,256]{2,1,0:T(8,128)S(1)}, f32[2,16,256]{2,1,0:T(8,128)S(1)}, u32[]{:S(2)}, u32[]{:S(2)}) collective-permute-start(f32[2,16,256]{2,1,0:T(8,128)S(1)} %get-tuple-element.45.stats.refs_0_), channel_id=1, source_target_pairs={{0,3},{1,2},{2,1},{3,0},{4,5},{5,4},{6,7},{7,6},{8,11},{9,10},{10,... | collective-permute-start | bytes 98312 | tf_op jit(solution)/shard_map/ppermute | solution.py:329
  49.6 1.2 %exps.1.before = f32[16,2,256,256]{3,2,1,0:T(8,128)S(1)} custom-call(f32[16,2,256,256]{3,2,1,0:T(8,128)S(1)} %get-tuple-element.44.score, f32[2,16,256]{2,1,0:T(8,128)S(1)} %get-tuple-element.45.stats.refs_0_), custom_call_target="tpu_custom_call" | custom-call | flops 8192 | bytes 1024 | tf_op jit(solution)/shard_map/exps/pallas_call | solution.py:37
  51.2 2.6 %collective-permute-done.11.refs_3_ = f32[2,16,256]{2,1,0:T(8,128)S(1)} collective-permute-done((f32[2,16,256]{2,1,0:T(8,128)S(1)}, f32[2,16,256]{2,1,0:T(8,128)S(1)}, u32[]{:S(2)}, u32[]{:S(2)}) %collective-permute-start.11) | collective-permute-done | bytes 32800 | tf_op jit(solution)/shard_map/ppermute | solution.py:329
  53.8 1.2 %column_0.1 = (f32[16,2,256,256]{3,2,1,0:T(8,128)S(1)}, f32[2,16,256]{2,1,0:T(8,128)S(1)}, f32[32,256]{1,0:T(8,128)S(1)}, f32[16,256]{1,0:T(8,128)S(1)}, f32[16,256]{1,0:T(8,128)S(1)}) custom-call(f32[32,256]{1,0:T(8,128)S(1)} %get-tuple-element.32.names.refs_0_, f32[16,2,256,256]{3,2,1,0:T(8,128)S(1)} %get-tuple-element.44.score, ...), custom_call_target="tpu_custom_call", output_to_operand_aliasing={{0}: (2, {})} | custom-call | flops 8192 | bytes 1024 | tf_op jit(solution)/shard_map/column_0/pallas_call | solution.py:37
  55.1 1.2 %collective-permute-done.12 = f32[2,16,256]{2,1,0:T(8,128)S(1)} collective-permute-done((f32[2,16,256]{2,1,0:T(8,128)S(1)}, f32[2,16,256]{2,1,0:T(8,128)S(1)}, u32[]{:S(2)}, u32[]{:S(2)}) %collective-permute-start.12) | collective-permute-done | bytes 32800 | tf_op jit(solution)/shard_map/ppermute | solution.py:295
  56.4 2.4 %collective-permute-start.13 = (f32[2,16,256]{2,1,0:T(8,128)S(1)}, f32[2,16,256]{2,1,0:T(8,128)S(1)}, u32[]{:S(2)}, u32[]{:S(2)}) collective-permute-start(f32[2,16,256]{2,1,0:T(8,128)S(1)} %broadcast_select_fusion.refs_0_), channel_id=1, source_target_pairs={{0,24},{1,25},{2,26},{3,27},{4,12},{5,13},{6,14},{7,15},{8,16},{9,... | collective-permute-start | bytes 98312 | tf_op jit(solution)/shard_map/ppermute | solution.py:329
  59.9 1.4 %collective-permute-done.13.refs_1_ = f32[2,16,256]{2,1,0:T(8,128)S(1)} collective-permute-done((f32[2,16,256]{2,1,0:T(8,128)S(1)}, f32[2,16,256]{2,1,0:T(8,128)S(1)}, u32[]{:S(2)}, u32[]{:S(2)}) %collective-permute-start.13) | collective-permute-done | bytes 32800 | tf_op jit(solution)/shard_map/ppermute | solution.py:329
  61.3 1.5 %collective-permute-done.14.refs_2_ = f32[2,16,256]{2,1,0:T(8,128)S(1)} collective-permute-done((f32[2,16,256]{2,1,0:T(8,128)S(1)}, f32[2,16,256]{2,1,0:T(8,128)S(1)}, u32[]{:S(2)}, u32[]{:S(2)}) %collective-permute-start.14) | collective-permute-done | bytes 32800 | tf_op jit(solution)/shard_map/ppermute | solution.py:329
  63.9 1.6 %collective-permute-start.16 = (f32[16,256]{1,0:T(8,128)S(1)}, f32[16,256]{1,0:T(8,128)S(1)}, u32[]{:S(2)}, u32[]{:S(2)}) collective-permute-start(f32[16,256]{1,0:T(8,128)S(1)} %get-tuple-element.52.refs_5_), channel_id=1, source_target_pairs={{0,3},{1,2},{2,1},{3,0},{4,5},{5,4},{6,7},{7,6},{8,11},{9,10},{10,... | collective-permute-start | bytes 49160 | tf_op jit(solution)/shard_map/ppermute | solution.py:329
  66.0 2.3 %collective-permute-start.18 = (f32[16,256]{1,0:T(8,128)S(1)}, f32[16,256]{1,0:T(8,128)S(1)}, u32[]{:S(2)}, u32[]{:S(2)}) collective-permute-start(f32[16,256]{1,0:T(8,128)S(1)} %get-tuple-element.52.refs_5_), channel_id=1, source_target_pairs={{0,1},{1,0},{2,3},{3,2},{4,6},{5,7},{6,4},{7,5},{8,9},{9,8},{10,11... | collective-permute-start | bytes 49160 | tf_op jit(solution)/shard_map/ppermute | solution.py:329
  71.2 1.2 %collective-permute-done.19 = f32[16,256]{1,0:T(8,128)S(1)} collective-permute-done((f32[16,256]{1,0:T(8,128)S(1)}, f32[16,256]{1,0:T(8,128)S(1)}, u32[]{:S(2)}, u32[]{:S(2)}) %collective-permute-start.19) | collective-permute-done | bytes 16416 | tf_op jit(solution)/shard_map/ppermute | solution.py:295
  72.4 1.6 %collective-permute-start.20 = (f32[16,256]{1,0:T(8,128)S(1)}, f32[16,256]{1,0:T(8,128)S(1)}, u32[]{:S(2)}, u32[]{:S(2)}) collective-permute-start(f32[16,256]{1,0:T(8,128)S(1)} %add.11.refs_0_), channel_id=1, source_target_pairs={{0,24},{1,25},{2,26},{3,27},{4,12},{5,13},{6,14},{7,15},{8,16},{9,... | collective-permute-start | bytes 49160 | tf_op jit(solution)/shard_map/ppermute | solution.py:329
  74.7 1.2 %collective-permute-start.22 = (f32[16,256]{1,0:T(8,128)S(1)}, f32[16,256]{1,0:T(8,128)S(1)}, u32[]{:S(2)}, u32[]{:S(2)}) collective-permute-start(f32[16,256]{1,0:T(8,128)S(1)} %add.11.refs_0_), channel_id=1, source_target_pairs={{0,8},{1,9},{2,10},{3,11},{4,20},{5,21},{6,22},{7,23},{8,0},{9,1},... | collective-permute-start | bytes 49160 | tf_op jit(solution)/shard_map/ppermute | solution.py:329
  79.2 2.2 %collective-permute-start.23 = (f32[16,256]{1,0:T(8,128)S(1)}, f32[16,256]{1,0:T(8,128)S(1)}, u32[]{:S(2)}, u32[]{:S(2)}) collective-permute-start(f32[16,256]{1,0:T(8,128)S(1)} %row_2.1.refs_6_), channel_id=1, source_target_pairs={{0,3},{1,2},{2,1},{3,0},{4,5},{5,4},{6,7},{7,6},{8,11},{9,10},{10,... | collective-permute-start | bytes 49160 | tf_op jit(solution)/shard_map/ppermute | solution.py:329
  82.4 1.3 %collective-permute-start.25 = (f32[16,256]{1,0:T(8,128)S(1)}, f32[16,256]{1,0:T(8,128)S(1)}, u32[]{:S(2)}, u32[]{:S(2)}) collective-permute-start(f32[16,256]{1,0:T(8,128)S(1)} %row_2.1.refs_6_), channel_id=1, source_target_pairs={{0,1},{1,0},{2,3},{3,2},{4,6},{5,7},{6,4},{7,5},{8,9},{9,8},{10,11... | collective-permute-start | bytes 49160 | tf_op jit(solution)/shard_map/ppermute | solution.py:329
  83.6 1.3 %collective-permute-done.23.refs_7_ = f32[16,256]{1,0:T(8,128)S(1)} collective-permute-done((f32[16,256]{1,0:T(8,128)S(1)}, f32[16,256]{1,0:T(8,128)S(1)}, u32[]{:S(2)}, u32[]{:S(2)}) %collective-permute-start.23) | collective-permute-done | bytes 16416 | tf_op jit(solution)/shard_map/ppermute | solution.py:329
  87.2 1.2 %collective-permute-done.26 = f32[16,256]{1,0:T(8,128)S(1)} collective-permute-done((f32[16,256]{1,0:T(8,128)S(1)}, f32[16,256]{1,0:T(8,128)S(1)}, u32[]{:S(2)}, u32[]{:S(2)}) %collective-permute-start.26) | collective-permute-done | bytes 16416 | tf_op jit(solution)/shard_map/ppermute | solution.py:295
  88.4 2.4 %collective-permute-start.27 = (f32[16,256]{1,0:T(8,128)S(1)}, f32[16,256]{1,0:T(8,128)S(1)}, u32[]{:S(2)}, u32[]{:S(2)}) collective-permute-start(f32[16,256]{1,0:T(8,128)S(1)} %add.12.refs_0_), channel_id=1, source_target_pairs={{0,24},{1,25},{2,26},{3,27},{4,12},{5,13},{6,14},{7,15},{8,16},{9,... | collective-permute-start | bytes 49160 | tf_op jit(solution)/shard_map/ppermute | solution.py:329
  93.0 1.5 %collective-permute-done.28.refs_2_ = f32[16,256]{1,0:T(8,128)S(1)} collective-permute-done((f32[16,256]{1,0:T(8,128)S(1)}, f32[16,256]{1,0:T(8,128)S(1)}, u32[]{:S(2)}, u32[]{:S(2)}) %collective-permute-start.28) | collective-permute-done | bytes 16416 | tf_op jit(solution)/shard_map/ppermute | solution.py:329
  (65 shorter events, 20.3 us)
Async XLA Ops:
  0.6 28.2 %copy-start.6 = (s32[16,2]{0,1:T(2,128)S(1)}, s32[16,2]{0,1:T(2,128)}, u32[]{:S(2)}) copy-start(s32[16,2]{0,1:T(2,128)} %param.10) | copy-start | bytes 388
  0.6 28.2 %copy-start.8 = (s32[16,1]{0,1:T(1,128)S(1)}, s32[16,1]{0,1:T(1,128)}, u32[]{:S(2)}) copy-start(s32[16,1]{0,1:T(1,128)} %param.11) | copy-start | bytes 196
  0.7 18.5 %collective-permute-start = (bf16[4096,128]{1,0:T(8,128)(2,1)}, bf16[4096,128]{1,0:T(8,128)(2,1)S(1)}, u32[]{:S(2)}, u32[]{:S(2)}) collective-permute-start(bf16[4096,128]{1,0:T(8,128)(2,1)} %refs_3_.1), channel_id=1, source_target_pairs={{0,8},{4,20},{8,0},{12,28},{16,24},{20,4},{24,16},{28,12},{1,9},{5... | collective-permute-start | bytes 3145736 | tf_op jit(solution)/shard_map/ppermute | solution.py:295
  3.7 25.1 %collective-permute-start.3 = (bf16[4096,128]{1,0:T(8,128)(2,1)}, bf16[4096,128]{1,0:T(8,128)(2,1)S(1)}, u32[]{:S(2)}, u32[]{:S(2)}) collective-permute-start(bf16[4096,128]{1,0:T(8,128)(2,1)} %refs_3_.1), channel_id=1, source_target_pairs={{0,4},{4,0},{8,12},{12,8},{16,20},{20,16},{24,28},{28,24},{1,5},{5... | collective-permute-start | bytes 3145736 | tf_op jit(solution)/shard_map/ppermute | solution.py:295
  12.0 15.1 %collective-permute-start.1 = (bf16[4096,128]{1,0:T(8,128)(2,1)S(1)}, bf16[4096,128]{1,0:T(8,128)(2,1)S(1)}, u32[]{:S(2)}, u32[]{:S(2)}) collective-permute-start(bf16[4096,128]{1,0:T(8,128)(2,1)S(1)} %copy-done.2), channel_id=1, source_target_pairs={{0,16},{4,12},{8,24},{12,4},{16,0},{20,28},{24,8},{28,20},{1,17},{... | collective-permute-start | bytes 3145736 | tf_op jit(solution)/shard_map/ppermute | solution.py:295
  19.2 9.6 %collective-permute-start.4 = (bf16[4096,128]{1,0:T(8,128)(2,1)S(1)}, bf16[4096,128]{1,0:T(8,128)(2,1)S(1)}, u32[]{:S(2)}, u32[]{:S(2)}) collective-permute-start(bf16[4096,128]{1,0:T(8,128)(2,1)S(1)} %collective-permute-done.refs_4_), channel_id=1, source_target_pairs={{0,4},{4,0},{8,12},{12,8},{16,20},{20,16},{24,28},{28,24},{1,5},{5... | collective-permute-start | bytes 3145736 | tf_op jit(solution)/shard_map/ppermute | solution.py:295
  19.2 13.8 %collective-permute-start.2 = (bf16[2048,128]{1,0:T(8,128)(2,1)S(1)}, bf16[2048,128]{1,0:T(8,128)(2,1)S(1)}, u32[]{:S(2)}, u32[]{:S(2)}) collective-permute-start(bf16[2048,128]{1,0:T(8,128)(2,1)S(1)} %get-tuple-element.57), channel_id=1, source_target_pairs={{0,16},{4,12},{8,24},{12,4},{16,0},{20,28},{24,8},{28,20},{1,17},{... | collective-permute-start | bytes 1572872 | tf_op jit(solution)/shard_map/ppermute | solution.py:295
  27.1 11.2 %collective-permute-start.6 = (bf16[2048,128]{1,0:T(8,128)(2,1)S(1)}, bf16[2048,128]{1,0:T(8,128)(2,1)S(1)}, u32[]{:S(2)}, u32[]{:S(2)}) collective-permute-start(bf16[2048,128]{1,0:T(8,128)(2,1)S(1)} %get-tuple-element.56), channel_id=1, source_target_pairs={{0,16},{4,12},{8,24},{12,4},{16,0},{20,28},{24,8},{28,20},{1,17},{... | collective-permute-start | bytes 1572872 | tf_op jit(solution)/shard_map/ppermute | solution.py:295
  33.1 5.2 %collective-permute-start.7 = (bf16[2048,128]{1,0:T(8,128)(2,1)S(1)}, bf16[2048,128]{1,0:T(8,128)(2,1)S(1)}, u32[]{:S(2)}, u32[]{:S(2)}) collective-permute-start(bf16[2048,128]{1,0:T(8,128)(2,1)S(1)} %collective-permute-done.2), channel_id=1, source_target_pairs={{0,4},{4,0},{8,12},{12,8},{16,20},{20,16},{24,28},{28,24},{1,5},{5... | collective-permute-start | bytes 1572872 | tf_op jit(solution)/shard_map/ppermute | solution.py:295
  34.0 6.5 %collective-permute-start.5 = (bf16[4096,128]{1,0:T(8,128)(2,1)S(1)}, bf16[4096,128]{1,0:T(8,128)(2,1)S(1)}, u32[]{:S(2)}, u32[]{:S(2)}) collective-permute-start(bf16[4096,128]{1,0:T(8,128)(2,1)S(1)} %collective-permute-done.1.refs_3_), channel_id=1, source_target_pairs={{0,4},{4,0},{8,12},{12,8},{16,20},{20,16},{24,28},{28,24},{1,5},{5... | collective-permute-start | bytes 3145736 | tf_op jit(solution)/shard_map/ppermute | solution.py:295
  38.3 2.2 %collective-permute-start.8 = (bf16[2048,128]{1,0:T(8,128)(2,1)S(1)}, bf16[2048,128]{1,0:T(8,128)(2,1)S(1)}, u32[]{:S(2)}, u32[]{:S(2)}) collective-permute-start(bf16[2048,128]{1,0:T(8,128)(2,1)S(1)} %collective-permute-done.6), channel_id=1, source_target_pairs={{0,4},{4,0},{8,12},{12,8},{16,20},{20,16},{24,28},{28,24},{1,5},{5... | collective-permute-start | bytes 1572872 | tf_op jit(solution)/shard_map/ppermute | solution.py:295
  44.7 6.4 %collective-permute-start.10 = (f32[2,16,256]{2,1,0:T(8,128)S(1)}, f32[2,16,256]{2,1,0:T(8,128)S(1)}, u32[]{:S(2)}, u32[]{:S(2)}) collective-permute-start(f32[2,16,256]{2,1,0:T(8,128)S(1)} %get-tuple-element.45.stats.refs_0_), channel_id=1, source_target_pairs={{0,3},{1,2},{2,1},{3,0},{4,5},{5,4},{6,7},{7,6},{8,11},{9,10},{10,... | collective-permute-start | bytes 98312 | tf_op jit(solution)/shard_map/ppermute | solution.py:329
  49.0 4.8 %collective-permute-start.11 = (f32[2,16,256]{2,1,0:T(8,128)S(1)}, f32[2,16,256]{2,1,0:T(8,128)S(1)}, u32[]{:S(2)}, u32[]{:S(2)}) collective-permute-start(f32[2,16,256]{2,1,0:T(8,128)S(1)} %get-tuple-element.45.stats.refs_0_), channel_id=1, source_target_pairs={{0,2},{1,3},{2,0},{3,1},{4,7},{5,6},{6,5},{7,4},{8,10},{9,11},{10,... | collective-permute-start | bytes 98312 | tf_op jit(solution)/shard_map/ppermute | solution.py:329
  49.0 4.8 %collective-permute-start.9 = (f32[2,16,256]{2,1,0:T(8,128)S(1)}, f32[2,16,256]{2,1,0:T(8,128)S(1)}, u32[]{:S(2)}, u32[]{:S(2)}) collective-permute-start(f32[2,16,256]{2,1,0:T(8,128)S(1)} %get-tuple-element.45.stats.refs_0_), channel_id=1, source_target_pairs={{0,1},{1,0},{2,3},{3,2},{4,6},{5,7},{6,4},{7,5},{8,9},{9,8},{10,11... | collective-permute-start | bytes 98312 | tf_op jit(solution)/shard_map/ppermute | solution.py:329
  55.0 1.3 %collective-permute-start.12 = (f32[2,16,256]{2,1,0:T(8,128)S(1)}, f32[2,16,256]{2,1,0:T(8,128)S(1)}, u32[]{:S(2)}, u32[]{:S(2)}) collective-permute-start(f32[2,16,256]{2,1,0:T(8,128)S(1)} %get-tuple-element.49), channel_id=1, source_target_pairs={{0,4},{4,0},{8,12},{12,8},{16,20},{20,16},{24,28},{28,24},{1,5},{5... | collective-permute-start | bytes 98312 | tf_op jit(solution)/shard_map/ppermute | solution.py:295
  56.4 4.9 %collective-permute-start.13 = (f32[2,16,256]{2,1,0:T(8,128)S(1)}, f32[2,16,256]{2,1,0:T(8,128)S(1)}, u32[]{:S(2)}, u32[]{:S(2)}) collective-permute-start(f32[2,16,256]{2,1,0:T(8,128)S(1)} %broadcast_select_fusion.refs_0_), channel_id=1, source_target_pairs={{0,24},{1,25},{2,26},{3,27},{4,12},{5,13},{6,14},{7,15},{8,16},{9,... | collective-permute-start | bytes 98312 | tf_op jit(solution)/shard_map/ppermute | solution.py:329
  58.8 3.9 %collective-permute-start.14 = (f32[2,16,256]{2,1,0:T(8,128)S(1)}, f32[2,16,256]{2,1,0:T(8,128)S(1)}, u32[]{:S(2)}, u32[]{:S(2)}) collective-permute-start(f32[2,16,256]{2,1,0:T(8,128)S(1)} %broadcast_select_fusion.refs_0_), channel_id=1, source_target_pairs={{0,16},{1,17},{2,18},{3,19},{4,28},{5,29},{6,30},{7,31},{8,24},{9,... | collective-permute-start | bytes 98312 | tf_op jit(solution)/shard_map/ppermute | solution.py:329
  59.2 3.9 %collective-permute-start.15 = (f32[2,16,256]{2,1,0:T(8,128)S(1)}, f32[2,16,256]{2,1,0:T(8,128)S(1)}, u32[]{:S(2)}, u32[]{:S(2)}) collective-permute-start(f32[2,16,256]{2,1,0:T(8,128)S(1)} %broadcast_select_fusion.refs_0_), channel_id=1, source_target_pairs={{0,8},{1,9},{2,10},{3,11},{4,20},{5,21},{6,22},{7,23},{8,0},{9,1},... | collective-permute-start | bytes 98312 | tf_op jit(solution)/shard_map/ppermute | solution.py:329
  63.9 5.6 %collective-permute-start.16 = (f32[16,256]{1,0:T(8,128)S(1)}, f32[16,256]{1,0:T(8,128)S(1)}, u32[]{:S(2)}, u32[]{:S(2)}) collective-permute-start(f32[16,256]{1,0:T(8,128)S(1)} %get-tuple-element.52.refs_5_), channel_id=1, source_target_pairs={{0,3},{1,2},{2,1},{3,0},{4,5},{5,4},{6,7},{7,6},{8,11},{9,10},{10,... | collective-permute-start | bytes 49160 | tf_op jit(solution)/shard_map/ppermute | solution.py:329
  65.6 4.7 %collective-permute-start.17 = (f32[16,256]{1,0:T(8,128)S(1)}, f32[16,256]{1,0:T(8,128)S(1)}, u32[]{:S(2)}, u32[]{:S(2)}) collective-permute-start(f32[16,256]{1,0:T(8,128)S(1)} %get-tuple-element.52.refs_5_), channel_id=1, source_target_pairs={{0,2},{1,3},{2,0},{3,1},{4,7},{5,6},{6,5},{7,4},{8,10},{9,11},{10,... | collective-permute-start | bytes 49160 | tf_op jit(solution)/shard_map/ppermute | solution.py:329
  66.0 4.2 %collective-permute-start.18 = (f32[16,256]{1,0:T(8,128)S(1)}, f32[16,256]{1,0:T(8,128)S(1)}, u32[]{:S(2)}, u32[]{:S(2)}) collective-permute-start(f32[16,256]{1,0:T(8,128)S(1)} %get-tuple-element.52.refs_5_), channel_id=1, source_target_pairs={{0,1},{1,0},{2,3},{3,2},{4,6},{5,7},{6,4},{7,5},{8,9},{9,8},{10,11... | collective-permute-start | bytes 49160 | tf_op jit(solution)/shard_map/ppermute | solution.py:329
  71.1 1.2 %collective-permute-start.19 = (f32[16,256]{1,0:T(8,128)S(1)}, f32[16,256]{1,0:T(8,128)S(1)}, u32[]{:S(2)}, u32[]{:S(2)}) collective-permute-start(f32[16,256]{1,0:T(8,128)S(1)} %column_1.1), channel_id=1, source_target_pairs={{0,4},{4,0},{8,12},{12,8},{16,20},{20,16},{24,28},{28,24},{1,5},{5... | collective-permute-start | bytes 49160 | tf_op jit(solution)/shard_map/ppermute | solution.py:295
  72.4 4.6 %collective-permute-start.20 = (f32[16,256]{1,0:T(8,128)S(1)}, f32[16,256]{1,0:T(8,128)S(1)}, u32[]{:S(2)}, u32[]{:S(2)}) collective-permute-start(f32[16,256]{1,0:T(8,128)S(1)} %add.11.refs_0_), channel_id=1, source_target_pairs={{0,24},{1,25},{2,26},{3,27},{4,12},{5,13},{6,14},{7,15},{8,16},{9,... | collective-permute-start | bytes 49160 | tf_op jit(solution)/shard_map/ppermute | solution.py:329
  74.0 3.8 %collective-permute-start.21 = (f32[16,256]{1,0:T(8,128)S(1)}, f32[16,256]{1,0:T(8,128)S(1)}, u32[]{:S(2)}, u32[]{:S(2)}) collective-permute-start(f32[16,256]{1,0:T(8,128)S(1)} %add.11.refs_0_), channel_id=1, source_target_pairs={{0,16},{1,17},{2,18},{3,19},{4,28},{5,29},{6,30},{7,31},{8,24},{9,... | collective-permute-start | bytes 49160 | tf_op jit(solution)/shard_map/ppermute | solution.py:329
  74.7 3.7 %collective-permute-start.22 = (f32[16,256]{1,0:T(8,128)S(1)}, f32[16,256]{1,0:T(8,128)S(1)}, u32[]{:S(2)}, u32[]{:S(2)}) collective-permute-start(f32[16,256]{1,0:T(8,128)S(1)} %add.11.refs_0_), channel_id=1, source_target_pairs={{0,8},{1,9},{2,10},{3,11},{4,20},{5,21},{6,22},{7,23},{8,0},{9,1},... | collective-permute-start | bytes 49160 | tf_op jit(solution)/shard_map/ppermute | solution.py:329
  79.2 5.7 %collective-permute-start.23 = (f32[16,256]{1,0:T(8,128)S(1)}, f32[16,256]{1,0:T(8,128)S(1)}, u32[]{:S(2)}, u32[]{:S(2)}) collective-permute-start(f32[16,256]{1,0:T(8,128)S(1)} %row_2.1.refs_6_), channel_id=1, source_target_pairs={{0,3},{1,2},{2,1},{3,0},{4,5},{5,4},{6,7},{7,6},{8,11},{9,10},{10,... | collective-permute-start | bytes 49160 | tf_op jit(solution)/shard_map/ppermute | solution.py:329
  81.4 4.6 %collective-permute-start.24 = (f32[16,256]{1,0:T(8,128)S(1)}, f32[16,256]{1,0:T(8,128)S(1)}, u32[]{:S(2)}, u32[]{:S(2)}) collective-permute-start(f32[16,256]{1,0:T(8,128)S(1)} %row_2.1.refs_6_), channel_id=1, source_target_pairs={{0,2},{1,3},{2,0},{3,1},{4,7},{5,6},{6,5},{7,4},{8,10},{9,11},{10,... | collective-permute-start | bytes 49160 | tf_op jit(solution)/shard_map/ppermute | solution.py:329
  82.4 3.9 %collective-permute-start.25 = (f32[16,256]{1,0:T(8,128)S(1)}, f32[16,256]{1,0:T(8,128)S(1)}, u32[]{:S(2)}, u32[]{:S(2)}) collective-permute-start(f32[16,256]{1,0:T(8,128)S(1)} %row_2.1.refs_6_), channel_id=1, source_target_pairs={{0,1},{1,0},{2,3},{3,2},{4,6},{5,7},{6,4},{7,5},{8,9},{9,8},{10,11... | collective-permute-start | bytes 49160 | tf_op jit(solution)/shard_map/ppermute | solution.py:329
  87.1 1.2 %collective-permute-start.26 = (f32[16,256]{1,0:T(8,128)S(1)}, f32[16,256]{1,0:T(8,128)S(1)}, u32[]{:S(2)}, u32[]{:S(2)}) collective-permute-start(f32[16,256]{1,0:T(8,128)S(1)} %get-tuple-element.55), channel_id=1, source_target_pairs={{0,4},{4,0},{8,12},{12,8},{16,20},{20,16},{24,28},{28,24},{1,5},{5... | collective-permute-start | bytes 49160 | tf_op jit(solution)/shard_map/ppermute | solution.py:295
  88.4 4.6 %collective-permute-start.27 = (f32[16,256]{1,0:T(8,128)S(1)}, f32[16,256]{1,0:T(8,128)S(1)}, u32[]{:S(2)}, u32[]{:S(2)}) collective-permute-start(f32[16,256]{1,0:T(8,128)S(1)} %add.12.refs_0_), channel_id=1, source_target_pairs={{0,24},{1,25},{2,26},{3,27},{4,12},{5,13},{6,14},{7,15},{8,16},{9,... | collective-permute-start | bytes 49160 | tf_op jit(solution)/shard_map/ppermute | solution.py:329
  90.8 3.7 %collective-permute-start.28 = (f32[16,256]{1,0:T(8,128)S(1)}, f32[16,256]{1,0:T(8,128)S(1)}, u32[]{:S(2)}, u32[]{:S(2)}) collective-permute-start(f32[16,256]{1,0:T(8,128)S(1)} %add.12.refs_0_), channel_id=1, source_target_pairs={{0,16},{1,17},{2,18},{3,19},{4,28},{5,29},{6,30},{7,31},{8,24},{9,... | collective-permute-start | bytes 49160 | tf_op jit(solution)/shard_map/ppermute | solution.py:329
  91.2 3.7 %collective-permute-start.29 = (f32[16,256]{1,0:T(8,128)S(1)}, f32[16,256]{1,0:T(8,128)S(1)}, u32[]{:S(2)}, u32[]{:S(2)}) collective-permute-start(f32[16,256]{1,0:T(8,128)S(1)} %add.12.refs_0_), channel_id=1, source_target_pairs={{0,8},{1,9},{2,10},{3,11},{4,20},{5,21},{6,22},{7,23},{8,0},{9,1},... | collective-permute-start | bytes 49160 | tf_op jit(solution)/shard_map/ppermute | solution.py:329
  (7 other events, 38.7 us)

commit v3 on v2

--- a/solution.py
+++ b/solution.py
@@ -307,26 +307,26 @@
 
 
 def exchange(x, axis, sizes, join, orders=((3, 1), (2, 3), (1, 2))):
-    n_row, n_col = sizes
-    n = n_row if axis == "row" else n_col
+    n = sizes[axis]
     if n & (n - 1):
         return [lax.all_gather(x, axis)[k] for k in range(n)]
-    low = 1
+    low, pairwise = 1, []
     while n // low not in (1, 4):
-        x = join([x, swap(x, axis, n, low)])
+        pairwise.append(low)
         low *= 2
-    if low == n:
-        return [x]
     mixed = axis == "col" or low > 1
     parts = [x]
-    for even, odd in orders:
+    for even, odd in orders if low < n else ():
         pairs = []
-        for row in range(n_row):
-            for col in range(n_col):
+        for row in range(sizes["row"]):
+            for col in range(sizes["col"]):
                 mask = low * (odd if mixed and row & 1 else even)
                 to = (row ^ mask, col) if axis == "row" else (row, col ^ mask)
-                pairs.append((row * n_col + col, to[0] * n_col + to[1]))
+                pairs.append((row * sizes["col"] + col, to[0] * sizes["col"] + to[1]))
         parts.append(lax.ppermute(x, ("row", "col"), pairs))
+    for mask in pairwise:
+        x = join(parts)
+        parts = [x, swap(x, axis, n, mask)]
     return parts
 
 
@@ -374,7 +374,7 @@
     index, count = tile_index.T, tile_count.T
     slot_rows = (tiles * slots, TILE)
     columns = (TILE, LANES)
-    sizes = (n_row, n_col)
+    sizes = {"row": n_row, "col": n_col}
 
     def score(before, pieces, last):
         operands = [index, count, source, *[piece for piece, _ in pieces]]

time: 95.8 us -> 95.8 us (level)
  no operation moved by 1% of the time
where the time goes in v3:
time: 95.8 us; the launch traced here: 95.6 us
  waiting for transfers between devices  36.8 us (38%)
  starting transfers between devices  33.9 us (35%)
  Pallas kernels  17.1 us (18%)
  local copies, waits for them, and re-layouts  6.63 us (7%)
    ppermute x18, starting transfers between devices, exchange(): parts.append(lax.ppermute(x, ('row', 'col'), pairs))  24.4 us
    ppermute x12, waiting for transfers between devices, permute(): return lax.ppermute(x, axis, [(i, partner(i)) for i in range(n)])  20.5 us
    pallas_call x10, Pallas kernels, kernel_call(): pl.pallas_call(body, out_shape=[(jax.ShapeDtypeStruct if final else VMEM)...  17.1 us
    ppermute x18, waiting for transfers between devices, exchange(): parts.append(lax.ppermute(x, ('row', 'col'), pairs))  16.4 us
    ppermute x12, starting transfers between devices, permute(): return lax.ppermute(x, axis, [(i, partner(i)) for i in range(n)])  9.58 us
    unnamed x19, local copies, waits for them, and re-layouts  6.57 us
  transfers between devices with their start and end apart: 30, of which 23 were waited for; matrix products, arithmetic and copies ran while one was open for 1% of the time, Pallas kernels for 8%

profile of v3, /device:TPU:0, one launch (start us, length us, event | category | flops | bytes accessed | tf_op | source)
XLA Modules:
  0.0 95.6 jit_solution(15915133289570505749)
XLA Ops:
  0.7 3.0 %collective-permute-start = (bf16[4096,128]{1,0:T(8,128)(2,1)}, bf16[4096,128]{1,0:T(8,128)(2,1)S(1)}, u32[]{:S(2)}, u32[]{:S(2)}) collective-permute-start(bf16[4096,128]{1,0:T(8,128)(2,1)} %refs_3_.1), channel_id=1, source_target_pairs={{0,8},{4,20},{8,0},{12,28},{16,24},{20,4},{24,16},{28,12},{1,9},{5... | collective-permute-start | bytes 3145736 | tf_op jit(solution)/shard_map/ppermute | solution.py:295
  3.7 3.4 %copy-done = bf16[4096,1024]{1,0:T(8,128)(2,1)S(1)} copy-done((bf16[4096,1024]{1,0:T(8,128)(2,1)S(1)}, bf16[4096,1024]{1,0:T(8,128)(2,1)}, u32[]{:S(2)}) %copy-start) | copy-done | bytes 8388632
  7.0 1.2 %copy-done.2 = bf16[4096,128]{1,0:T(8,128)(2,1)S(1)} copy-done((bf16[4096,128]{1,0:T(8,128)(2,1)S(1)}, bf16[4096,128]{1,0:T(8,128)(2,1)}, u32[]{:S(2)}) %copy-start.2) | copy-done | bytes 1048600
  9.6 2.4 %score_1_False.1 = (f32[16,2,256,256]{3,2,1,0:T(8,128)S(1)}, f32[32,256]{1,0:T(8,128)S(1)}) custom-call(s32[2,16]{1,0:T(2,128)S(1)} %bitcast.17, s32[1,16]{1,0:T(1,128)S(1)} %bitcast.20, bf16[4096,1024]{1,0:T(8,128)(2,1)S(1)} %copy-done, bf16[4096,128]{1,0:T(8,128)(2,1)S(1)} %copy-done.2), custom_call_target="tpu_custom_call" | custom-call | flops 8192 | bytes 1024 | tf_op jit(solution)/shard_map/score_1_False/pallas_call | solution.py:37
  12.0 1.6 %collective-permute-start.1 = (bf16[4096,128]{1,0:T(8,128)(2,1)S(1)}, bf16[4096,128]{1,0:T(8,128)(2,1)S(1)}, u32[]{:S(2)}, u32[]{:S(2)}) collective-permute-start(bf16[4096,128]{1,0:T(8,128)(2,1)S(1)} %copy-done.2), channel_id=1, source_target_pairs={{0,16},{4,12},{8,24},{12,4},{16,0},{20,28},{24,8},{28,20},{1,17},{... | collective-permute-start | bytes 3145736 | tf_op jit(solution)/shard_map/ppermute | solution.py:295
  13.6 5.6 %collective-permute-done.refs_4_ = bf16[4096,128]{1,0:T(8,128)(2,1)S(1)} collective-permute-done((bf16[4096,128]{1,0:T(8,128)(2,1)}, bf16[4096,128]{1,0:T(8,128)(2,1)S(1)}, u32[]{:S(2)}, u32[]{:S(2)}) %collective-permute-start) | collective-permute-done | bytes 1048608 | tf_op jit(solution)/shard_map/ppermute | solution.py:295
  19.2 1.6 %collective-permute-start.2 = (bf16[2048,128]{1,0:T(8,128)(2,1)S(1)}, bf16[2048,128]{1,0:T(8,128)(2,1)S(1)}, u32[]{:S(2)}, u32[]{:S(2)}) collective-permute-start(bf16[2048,128]{1,0:T(8,128)(2,1)S(1)} %get-tuple-element.57), channel_id=1, source_target_pairs={{0,16},{4,12},{8,24},{12,4},{16,0},{20,28},{24,8},{28,20},{1,17},{... | collective-permute-start | bytes 1572872 | tf_op jit(solution)/shard_map/ppermute | solution.py:295
  20.9 6.2 %collective-permute-done.1.refs_3_ = bf16[4096,128]{1,0:T(8,128)(2,1)S(1)} collective-permute-done((bf16[4096,128]{1,0:T(8,128)(2,1)S(1)}, bf16[4096,128]{1,0:T(8,128)(2,1)S(1)}, u32[]{:S(2)}, u32[]{:S(2)}) %collective-permute-start.1) | collective-permute-done | bytes 1048608 | tf_op jit(solution)/shard_map/ppermute | solution.py:295
  27.1 1.7 %collective-permute-start.6 = (bf16[2048,128]{1,0:T(8,128)(2,1)S(1)}, bf16[2048,128]{1,0:T(8,128)(2,1)S(1)}, u32[]{:S(2)}, u32[]{:S(2)}) collective-permute-start(bf16[2048,128]{1,0:T(8,128)(2,1)S(1)} %get-tuple-element.56), channel_id=1, source_target_pairs={{0,16},{4,12},{8,24},{12,4},{16,0},{20,28},{24,8},{28,20},{1,17},{... | collective-permute-start | bytes 1572872 | tf_op jit(solution)/shard_map/ppermute | solution.py:295
  28.8 4.3 %score_3_False.1 = (f32[16,2,256,256]{3,2,1,0:T(8,128)S(1)}, f32[8,128]{1,0:T(8,128)}) custom-call(s32[2,16]{1,0:T(2,128)S(1)} %bitcast.18, s32[1,16]{1,0:T(1,128)S(1)} %bitcast.21, bf16[4096,1024]{1,0:T(8,128)(2,1)S(1)} %copy-done.1, bf16[4096,128]{1,0:T(8,128)(2,1)S(1)} %collective-permute-done.3.refs_3_, ...), custom_call_target="tpu_custom_call" | custom-call | flops 8192 | bytes 1024 | tf_op jit(solution)/shard_map/score_3_False/pallas_call | solution.py:37
  34.0 4.3 %collective-permute-done.6 = bf16[2048,128]{1,0:T(8,128)(2,1)S(1)} collective-permute-done((bf16[2048,128]{1,0:T(8,128)(2,1)S(1)}, bf16[2048,128]{1,0:T(8,128)(2,1)S(1)}, u32[]{:S(2)}, u32[]{:S(2)}) %collective-permute-start.6) | collective-permute-done | bytes 524320 | tf_op jit(solution)/shard_map/ppermute | solution.py:295
  39.0 1.5 %collective-permute-done.8 = bf16[2048,128]{1,0:T(8,128)(2,1)S(1)} collective-permute-done((bf16[2048,128]{1,0:T(8,128)(2,1)S(1)}, bf16[2048,128]{1,0:T(8,128)(2,1)S(1)}, u32[]{:S(2)}, u32[]{:S(2)}) %collective-permute-start.8) | collective-permute-done | bytes 524320 | tf_op jit(solution)/shard_map/ppermute | solution.py:295
  40.6 4.2 %score_4_True.1 = (f32[16,2,256,256]{3,2,1,0:T(8,128)S(1)}, f32[2,16,256]{2,1,0:T(8,128)S(1)}) custom-call(s32[2,16]{1,0:T(2,128)S(1)} %bitcast.19, s32[1,16]{1,0:T(1,128)S(1)} %bitcast.22, bf16[4096,1024]{1,0:T(8,128)(2,1)S(1)} %copy-done.1, bf16[4096,128]{1,0:T(8,128)(2,1)S(1)} %collective-permute-done.1.refs_3_, ...), custom_call_target="tpu_custom_call" | custom-call | flops 8192 | bytes 1024 | tf_op jit(solution)/shard_map/score_4_True/pallas_call | solution.py:37
  44.7 4.2 %collective-permute-start.10 = (f32[2,16,256]{2,1,0:T(8,128)S(1)}, f32[2,16,256]{2,1,0:T(8,128)S(1)}, u32[]{:S(2)}, u32[]{:S(2)}) collective-permute-start(f32[2,16,256]{2,1,0:T(8,128)S(1)} %get-tuple-element.45.stats.refs_0_), channel_id=1, source_target_pairs={{0,3},{1,2},{2,1},{3,0},{4,5},{5,4},{6,7},{7,6},{8,11},{9,10},{10,... | collective-permute-start | bytes 98312 | tf_op jit(solution)/shard_map/ppermute | solution.py:326
  49.6 1.2 %exps.1.before = f32[16,2,256,256]{3,2,1,0:T(8,128)S(1)} custom-call(f32[16,2,256,256]{3,2,1,0:T(8,128)S(1)} %get-tuple-element.44.score, f32[2,16,256]{2,1,0:T(8,128)S(1)} %get-tuple-element.45.stats.refs_0_), custom_call_target="tpu_custom_call" | custom-call | flops 8192 | bytes 1024 | tf_op jit(solution)/shard_map/exps/pallas_call | solution.py:37
  51.2 2.6 %collective-permute-done.11.refs_3_ = f32[2,16,256]{2,1,0:T(8,128)S(1)} collective-permute-done((f32[2,16,256]{2,1,0:T(8,128)S(1)}, f32[2,16,256]{2,1,0:T(8,128)S(1)}, u32[]{:S(2)}, u32[]{:S(2)}) %collective-permute-start.11) | collective-permute-done | bytes 32800 | tf_op jit(solution)/shard_map/ppermute | solution.py:326
  53.8 1.2 %column_0.1 = (f32[16,2,256,256]{3,2,1,0:T(8,128)S(1)}, f32[2,16,256]{2,1,0:T(8,128)S(1)}, f32[32,256]{1,0:T(8,128)S(1)}, f32[16,256]{1,0:T(8,128)S(1)}, f32[16,256]{1,0:T(8,128)S(1)}) custom-call(f32[32,256]{1,0:T(8,128)S(1)} %get-tuple-element.32.names.refs_0_, f32[16,2,256,256]{3,2,1,0:T(8,128)S(1)} %get-tuple-element.44.score, ...), custom_call_target="tpu_custom_call", output_to_operand_aliasing={{0}: (2, {})} | custom-call | flops 8192 | bytes 1024 | tf_op jit(solution)/shard_map/column_0/pallas_call | solution.py:37
  55.0 2.5 %collective-permute-start.12 = (f32[2,16,256]{2,1,0:T(8,128)S(1)}, f32[2,16,256]{2,1,0:T(8,128)S(1)}, u32[]{:S(2)}, u32[]{:S(2)}) collective-permute-start(f32[2,16,256]{2,1,0:T(8,128)S(1)} %get-tuple-element.49), channel_id=1, source_target_pairs={{0,24},{1,25},{2,26},{3,27},{4,12},{5,13},{6,14},{7,15},{8,16},{9,... | collective-permute-start | bytes 98312 | tf_op jit(solution)/shard_map/ppermute | solution.py:326
  58.6 1.6 %collective-permute-done.12 = f32[2,16,256]{2,1,0:T(8,128)S(1)} collective-permute-done((f32[2,16,256]{2,1,0:T(8,128)S(1)}, f32[2,16,256]{2,1,0:T(8,128)S(1)}, u32[]{:S(2)}, u32[]{:S(2)}) %collective-permute-start.12) | collective-permute-done | bytes 32800 | tf_op jit(solution)/shard_map/ppermute | solution.py:326
  60.2 1.2 %collective-permute-done.13 = f32[2,16,256]{2,1,0:T(8,128)S(1)} collective-permute-done((f32[2,16,256]{2,1,0:T(8,128)S(1)}, f32[2,16,256]{2,1,0:T(8,128)S(1)}, u32[]{:S(2)}, u32[]{:S(2)}) %collective-permute-start.13) | collective-permute-done | bytes 32800 | tf_op jit(solution)/shard_map/ppermute | solution.py:326
  62.0 1.2 %collective-permute-done.15.refs_1_ = f32[2,16,256]{2,1,0:T(8,128)S(1)} collective-permute-done((f32[2,16,256]{2,1,0:T(8,128)S(1)}, f32[2,16,256]{2,1,0:T(8,128)S(1)}, u32[]{:S(2)}, u32[]{:S(2)}) %collective-permute-start.15) | collective-permute-done | bytes 32800 | tf_op jit(solution)/shard_map/ppermute | solution.py:295
  63.9 1.6 %collective-permute-start.16 = (f32[16,256]{1,0:T(8,128)S(1)}, f32[16,256]{1,0:T(8,128)S(1)}, u32[]{:S(2)}, u32[]{:S(2)}) collective-permute-start(f32[16,256]{1,0:T(8,128)S(1)} %get-tuple-element.52.refs_5_), channel_id=1, source_target_pairs={{0,3},{1,2},{2,1},{3,0},{4,5},{5,4},{6,7},{7,6},{8,11},{9,10},{10,... | collective-permute-start | bytes 49160 | tf_op jit(solution)/shard_map/ppermute | solution.py:326
  66.0 2.3 %collective-permute-start.18 = (f32[16,256]{1,0:T(8,128)S(1)}, f32[16,256]{1,0:T(8,128)S(1)}, u32[]{:S(2)}, u32[]{:S(2)}) collective-permute-start(f32[16,256]{1,0:T(8,128)S(1)} %get-tuple-element.52.refs_5_), channel_id=1, source_target_pairs={{0,1},{1,0},{2,3},{3,2},{4,6},{5,7},{6,4},{7,5},{8,9},{9,8},{10,11... | collective-permute-start | bytes 49160 | tf_op jit(solution)/shard_map/ppermute | solution.py:326
  68.4 1.3 %collective-permute-done.16.refs_6_ = f32[16,256]{1,0:T(8,128)S(1)} collective-permute-done((f32[16,256]{1,0:T(8,128)S(1)}, f32[16,256]{1,0:T(8,128)S(1)}, u32[]{:S(2)}, u32[]{:S(2)}) %collective-permute-start.16) | collective-permute-done | bytes 16416 | tf_op jit(solution)/shard_map/ppermute | solution.py:326
  71.1 1.6 %collective-permute-start.19 = (f32[16,256]{1,0:T(8,128)S(1)}, f32[16,256]{1,0:T(8,128)S(1)}, u32[]{:S(2)}, u32[]{:S(2)}) collective-permute-start(f32[16,256]{1,0:T(8,128)S(1)} %column_1.1), channel_id=1, source_target_pairs={{0,24},{1,25},{2,26},{3,27},{4,12},{5,13},{6,14},{7,15},{8,16},{9,... | collective-permute-start | bytes 49160 | tf_op jit(solution)/shard_map/ppermute | solution.py:326
  73.3 1.4 %collective-permute-start.21 = (f32[16,256]{1,0:T(8,128)S(1)}, f32[16,256]{1,0:T(8,128)S(1)}, u32[]{:S(2)}, u32[]{:S(2)}) collective-permute-start(f32[16,256]{1,0:T(8,128)S(1)} %column_1.1), channel_id=1, source_target_pairs={{0,8},{1,9},{2,10},{3,11},{4,20},{5,21},{6,22},{7,23},{8,0},{9,1},... | collective-permute-start | bytes 49160 | tf_op jit(solution)/shard_map/ppermute | solution.py:326
  77.1 1.2 %collective-permute-done.22.refs_1_ = f32[16,256]{1,0:T(8,128)S(1)} collective-permute-done((f32[16,256]{1,0:T(8,128)S(1)}, f32[16,256]{1,0:T(8,128)S(1)}, u32[]{:S(2)}, u32[]{:S(2)}) %collective-permute-start.22) | collective-permute-done | bytes 16416 | tf_op jit(solution)/shard_map/ppermute | solution.py:295
  79.0 2.4 %collective-permute-start.23 = (f32[16,256]{1,0:T(8,128)S(1)}, f32[16,256]{1,0:T(8,128)S(1)}, u32[]{:S(2)}, u32[]{:S(2)}) collective-permute-start(f32[16,256]{1,0:T(8,128)S(1)} %row_2.1.refs_6_), channel_id=1, source_target_pairs={{0,3},{1,2},{2,1},{3,0},{4,5},{5,4},{6,7},{7,6},{8,11},{9,10},{10,... | collective-permute-start | bytes 49160 | tf_op jit(solution)/shard_map/ppermute | solution.py:326
  84.6 1.5 %collective-permute-done.24.refs_8_ = f32[16,256]{1,0:T(8,128)S(1)} collective-permute-done((f32[16,256]{1,0:T(8,128)S(1)}, f32[16,256]{1,0:T(8,128)S(1)}, u32[]{:S(2)}, u32[]{:S(2)}) %collective-permute-start.24) | collective-permute-done | bytes 16416 | tf_op jit(solution)/shard_map/ppermute | solution.py:326
  87.1 2.5 %collective-permute-start.26 = (f32[16,256]{1,0:T(8,128)S(1)}, f32[16,256]{1,0:T(8,128)S(1)}, u32[]{:S(2)}, u32[]{:S(2)}) collective-permute-start(f32[16,256]{1,0:T(8,128)S(1)} %get-tuple-element.55), channel_id=1, source_target_pairs={{0,24},{1,25},{2,26},{3,27},{4,12},{5,13},{6,14},{7,15},{8,16},{9,... | collective-permute-start | bytes 49160 | tf_op jit(solution)/shard_map/ppermute | solution.py:326
  90.7 1.2 %collective-permute-done.26 = f32[16,256]{1,0:T(8,128)S(1)} collective-permute-done((f32[16,256]{1,0:T(8,128)S(1)}, f32[16,256]{1,0:T(8,128)S(1)}, u32[]{:S(2)}, u32[]{:S(2)}) %collective-permute-start.26) | collective-permute-done | bytes 16416 | tf_op jit(solution)/shard_map/ppermute | solution.py:326
  91.8 1.5 %collective-permute-done.27 = f32[16,256]{1,0:T(8,128)S(1)} collective-permute-done((f32[16,256]{1,0:T(8,128)S(1)}, f32[16,256]{1,0:T(8,128)S(1)}, u32[]{:S(2)}, u32[]{:S(2)}) %collective-permute-start.27) | collective-permute-done | bytes 16416 | tf_op jit(solution)/shard_map/ppermute | solution.py:326
  (65 shorter events, 19.8 us)
Async XLA Ops:
  0.6 28.2 %copy-start.6 = (s32[16,2]{0,1:T(2,128)S(1)}, s32[16,2]{0,1:T(2,128)}, u32[]{:S(2)}) copy-start(s32[16,2]{0,1:T(2,128)} %param.10) | copy-start | bytes 388
  0.6 28.2 %copy-start.8 = (s32[16,1]{0,1:T(1,128)S(1)}, s32[16,1]{0,1:T(1,128)}, u32[]{:S(2)}) copy-start(s32[16,1]{0,1:T(1,128)} %param.11) | copy-start | bytes 196
  0.7 18.5 %collective-permute-start = (bf16[4096,128]{1,0:T(8,128)(2,1)}, bf16[4096,128]{1,0:T(8,128)(2,1)S(1)}, u32[]{:S(2)}, u32[]{:S(2)}) collective-permute-start(bf16[4096,128]{1,0:T(8,128)(2,1)} %refs_3_.1), channel_id=1, source_target_pairs={{0,8},{4,20},{8,0},{12,28},{16,24},{20,4},{24,16},{28,12},{1,9},{5... | collective-permute-start | bytes 3145736 | tf_op jit(solution)/shard_map/ppermute | solution.py:295
  3.7 25.1 %collective-permute-start.3 = (bf16[4096,128]{1,0:T(8,128)(2,1)}, bf16[4096,128]{1,0:T(8,128)(2,1)S(1)}, u32[]{:S(2)}, u32[]{:S(2)}) collective-permute-start(bf16[4096,128]{1,0:T(8,128)(2,1)} %refs_3_.1), channel_id=1, source_target_pairs={{0,4},{4,0},{8,12},{12,8},{16,20},{20,16},{24,28},{28,24},{1,5},{5... | collective-permute-start | bytes 3145736 | tf_op jit(solution)/shard_map/ppermute | solution.py:295
  12.0 15.1 %collective-permute-start.1 = (bf16[4096,128]{1,0:T(8,128)(2,1)S(1)}, bf16[4096,128]{1,0:T(8,128)(2,1)S(1)}, u32[]{:S(2)}, u32[]{:S(2)}) collective-permute-start(bf16[4096,128]{1,0:T(8,128)(2,1)S(1)} %copy-done.2), channel_id=1, source_target_pairs={{0,16},{4,12},{8,24},{12,4},{16,0},{20,28},{24,8},{28,20},{1,17},{... | collective-permute-start | bytes 3145736 | tf_op jit(solution)/shard_map/ppermute | solution.py:295
  19.2 9.6 %collective-permute-start.4 = (bf16[4096,128]{1,0:T(8,128)(2,1)S(1)}, bf16[4096,128]{1,0:T(8,128)(2,1)S(1)}, u32[]{:S(2)}, u32[]{:S(2)}) collective-permute-start(bf16[4096,128]{1,0:T(8,128)(2,1)S(1)} %collective-permute-done.refs_4_), channel_id=1, source_target_pairs={{0,4},{4,0},{8,12},{12,8},{16,20},{20,16},{24,28},{28,24},{1,5},{5... | collective-permute-start | bytes 3145736 | tf_op jit(solution)/shard_map/ppermute | solution.py:295
  19.2 13.8 %collective-permute-start.2 = (bf16[2048,128]{1,0:T(8,128)(2,1)S(1)}, bf16[2048,128]{1,0:T(8,128)(2,1)S(1)}, u32[]{:S(2)}, u32[]{:S(2)}) collective-permute-start(bf16[2048,128]{1,0:T(8,128)(2,1)S(1)} %get-tuple-element.57), channel_id=1, source_target_pairs={{0,16},{4,12},{8,24},{12,4},{16,0},{20,28},{24,8},{28,20},{1,17},{... | collective-permute-start | bytes 1572872 | tf_op jit(solution)/shard_map/ppermute | solution.py:295
  27.1 11.2 %collective-permute-start.6 = (bf16[2048,128]{1,0:T(8,128)(2,1)S(1)}, bf16[2048,128]{1,0:T(8,128)(2,1)S(1)}, u32[]{:S(2)}, u32[]{:S(2)}) collective-permute-start(bf16[2048,128]{1,0:T(8,128)(2,1)S(1)} %get-tuple-element.56), channel_id=1, source_target_pairs={{0,16},{4,12},{8,24},{12,4},{16,0},{20,28},{24,8},{28,20},{1,17},{... | collective-permute-start | bytes 1572872 | tf_op jit(solution)/shard_map/ppermute | solution.py:295
  33.1 5.2 %collective-permute-start.7 = (bf16[2048,128]{1,0:T(8,128)(2,1)S(1)}, bf16[2048,128]{1,0:T(8,128)(2,1)S(1)}, u32[]{:S(2)}, u32[]{:S(2)}) collective-permute-start(bf16[2048,128]{1,0:T(8,128)(2,1)S(1)} %collective-permute-done.2), channel_id=1, source_target_pairs={{0,4},{4,0},{8,12},{12,8},{16,20},{20,16},{24,28},{28,24},{1,5},{5... | collective-permute-start | bytes 1572872 | tf_op jit(solution)/shard_map/ppermute | solution.py:295
  34.0 6.5 %collective-permute-start.5 = (bf16[4096,128]{1,0:T(8,128)(2,1)S(1)}, bf16[4096,128]{1,0:T(8,128)(2,1)S(1)}, u32[]{:S(2)}, u32[]{:S(2)}) collective-permute-start(bf16[4096,128]{1,0:T(8,128)(2,1)S(1)} %collective-permute-done.1.refs_3_), channel_id=1, source_target_pairs={{0,4},{4,0},{8,12},{12,8},{16,20},{20,16},{24,28},{28,24},{1,5},{5... | collective-permute-start | bytes 3145736 | tf_op jit(solution)/shard_map/ppermute | solution.py:295
  38.3 2.2 %collective-permute-start.8 = (bf16[2048,128]{1,0:T(8,128)(2,1)S(1)}, bf16[2048,128]{1,0:T(8,128)(2,1)S(1)}, u32[]{:S(2)}, u32[]{:S(2)}) collective-permute-start(bf16[2048,128]{1,0:T(8,128)(2,1)S(1)} %collective-permute-done.6), channel_id=1, source_target_pairs={{0,4},{4,0},{8,12},{12,8},{16,20},{20,16},{24,28},{28,24},{1,5},{5... | collective-permute-start | bytes 1572872 | tf_op jit(solution)/shard_map/ppermute | solution.py:295
  44.7 6.4 %collective-permute-start.10 = (f32[2,16,256]{2,1,0:T(8,128)S(1)}, f32[2,16,256]{2,1,0:T(8,128)S(1)}, u32[]{:S(2)}, u32[]{:S(2)}) collective-permute-start(f32[2,16,256]{2,1,0:T(8,128)S(1)} %get-tuple-element.45.stats.refs_0_), channel_id=1, source_target_pairs={{0,3},{1,2},{2,1},{3,0},{4,5},{5,4},{6,7},{7,6},{8,11},{9,10},{10,... | collective-permute-start | bytes 98312 | tf_op jit(solution)/shard_map/ppermute | solution.py:326
  49.0 4.8 %collective-permute-start.11 = (f32[2,16,256]{2,1,0:T(8,128)S(1)}, f32[2,16,256]{2,1,0:T(8,128)S(1)}, u32[]{:S(2)}, u32[]{:S(2)}) collective-permute-start(f32[2,16,256]{2,1,0:T(8,128)S(1)} %get-tuple-element.45.stats.refs_0_), channel_id=1, source_target_pairs={{0,2},{1,3},{2,0},{3,1},{4,7},{5,6},{6,5},{7,4},{8,10},{9,11},{10,... | collective-permute-start | bytes 98312 | tf_op jit(solution)/shard_map/ppermute | solution.py:326
  49.0 4.8 %collective-permute-start.9 = (f32[2,16,256]{2,1,0:T(8,128)S(1)}, f32[2,16,256]{2,1,0:T(8,128)S(1)}, u32[]{:S(2)}, u32[]{:S(2)}) collective-permute-start(f32[2,16,256]{2,1,0:T(8,128)S(1)} %get-tuple-element.45.stats.refs_0_), channel_id=1, source_target_pairs={{0,1},{1,0},{2,3},{3,2},{4,6},{5,7},{6,4},{7,5},{8,9},{9,8},{10,11... | collective-permute-start | bytes 98312 | tf_op jit(solution)/shard_map/ppermute | solution.py:326
  55.0 5.2 %collective-permute-start.12 = (f32[2,16,256]{2,1,0:T(8,128)S(1)}, f32[2,16,256]{2,1,0:T(8,128)S(1)}, u32[]{:S(2)}, u32[]{:S(2)}) collective-permute-start(f32[2,16,256]{2,1,0:T(8,128)S(1)} %get-tuple-element.49), channel_id=1, source_target_pairs={{0,24},{1,25},{2,26},{3,27},{4,12},{5,13},{6,14},{7,15},{8,16},{9,... | collective-permute-start | bytes 98312 | tf_op jit(solution)/shard_map/ppermute | solution.py:326
  57.5 3.9 %collective-permute-start.13 = (f32[2,16,256]{2,1,0:T(8,128)S(1)}, f32[2,16,256]{2,1,0:T(8,128)S(1)}, u32[]{:S(2)}, u32[]{:S(2)}) collective-permute-start(f32[2,16,256]{2,1,0:T(8,128)S(1)} %get-tuple-element.49), channel_id=1, source_target_pairs={{0,16},{1,17},{2,18},{3,19},{4,28},{5,29},{6,30},{7,31},{8,24},{9,... | collective-permute-start | bytes 98312 | tf_op jit(solution)/shard_map/ppermute | solution.py:326
  57.9 3.9 %collective-permute-start.14 = (f32[2,16,256]{2,1,0:T(8,128)S(1)}, f32[2,16,256]{2,1,0:T(8,128)S(1)}, u32[]{:S(2)}, u32[]{:S(2)}) collective-permute-start(f32[2,16,256]{2,1,0:T(8,128)S(1)} %get-tuple-element.49), channel_id=1, source_target_pairs={{0,8},{1,9},{2,10},{3,11},{4,20},{5,21},{6,22},{7,23},{8,0},{9,1},... | collective-permute-start | bytes 98312 | tf_op jit(solution)/shard_map/ppermute | solution.py:326
  61.9 1.2 %collective-permute-start.15 = (f32[2,16,256]{2,1,0:T(8,128)S(1)}, f32[2,16,256]{2,1,0:T(8,128)S(1)}, u32[]{:S(2)}, u32[]{:S(2)}) collective-permute-start(f32[2,16,256]{2,1,0:T(8,128)S(1)} %broadcast_select_fusion.refs_0_), channel_id=1, source_target_pairs={{0,4},{4,0},{8,12},{12,8},{16,20},{20,16},{24,28},{28,24},{1,5},{5... | collective-permute-start | bytes 98312 | tf_op jit(solution)/shard_map/ppermute | solution.py:295
  63.9 5.7 %collective-permute-start.16 = (f32[16,256]{1,0:T(8,128)S(1)}, f32[16,256]{1,0:T(8,128)S(1)}, u32[]{:S(2)}, u32[]{:S(2)}) collective-permute-start(f32[16,256]{1,0:T(8,128)S(1)} %get-tuple-element.52.refs_5_), channel_id=1, source_target_pairs={{0,3},{1,2},{2,1},{3,0},{4,5},{5,4},{6,7},{7,6},{8,11},{9,10},{10,... | collective-permute-start | bytes 49160 | tf_op jit(solution)/shard_map/ppermute | solution.py:326
  65.6 4.7 %collective-permute-start.17 = (f32[16,256]{1,0:T(8,128)S(1)}, f32[16,256]{1,0:T(8,128)S(1)}, u32[]{:S(2)}, u32[]{:S(2)}) collective-permute-start(f32[16,256]{1,0:T(8,128)S(1)} %get-tuple-element.52.refs_5_), channel_id=1, source_target_pairs={{0,2},{1,3},{2,0},{3,1},{4,7},{5,6},{6,5},{7,4},{8,10},{9,11},{10,... | collective-permute-start | bytes 49160 | tf_op jit(solution)/shard_map/ppermute | solution.py:326
  66.0 4.2 %collective-permute-start.18 = (f32[16,256]{1,0:T(8,128)S(1)}, f32[16,256]{1,0:T(8,128)S(1)}, u32[]{:S(2)}, u32[]{:S(2)}) collective-permute-start(f32[16,256]{1,0:T(8,128)S(1)} %get-tuple-element.52.refs_5_), channel_id=1, source_target_pairs={{0,1},{1,0},{2,3},{3,2},{4,6},{5,7},{6,4},{7,5},{8,9},{9,8},{10,11... | collective-permute-start | bytes 49160 | tf_op jit(solution)/shard_map/ppermute | solution.py:326
  71.1 4.7 %collective-permute-start.19 = (f32[16,256]{1,0:T(8,128)S(1)}, f32[16,256]{1,0:T(8,128)S(1)}, u32[]{:S(2)}, u32[]{:S(2)}) collective-permute-start(f32[16,256]{1,0:T(8,128)S(1)} %column_1.1), channel_id=1, source_target_pairs={{0,24},{1,25},{2,26},{3,27},{4,12},{5,13},{6,14},{7,15},{8,16},{9,... | collective-permute-start | bytes 49160 | tf_op jit(solution)/shard_map/ppermute | solution.py:326
  72.7 3.7 %collective-permute-start.20 = (f32[16,256]{1,0:T(8,128)S(1)}, f32[16,256]{1,0:T(8,128)S(1)}, u32[]{:S(2)}, u32[]{:S(2)}) collective-permute-start(f32[16,256]{1,0:T(8,128)S(1)} %column_1.1), channel_id=1, source_target_pairs={{0,16},{1,17},{2,18},{3,19},{4,28},{5,29},{6,30},{7,31},{8,24},{9,... | collective-permute-start | bytes 49160 | tf_op jit(solution)/shard_map/ppermute | solution.py:326
  73.3 3.7 %collective-permute-start.21 = (f32[16,256]{1,0:T(8,128)S(1)}, f32[16,256]{1,0:T(8,128)S(1)}, u32[]{:S(2)}, u32[]{:S(2)}) collective-permute-start(f32[16,256]{1,0:T(8,128)S(1)} %column_1.1), channel_id=1, source_target_pairs={{0,8},{1,9},{2,10},{3,11},{4,20},{5,21},{6,22},{7,23},{8,0},{9,1},... | collective-permute-start | bytes 49160 | tf_op jit(solution)/shard_map/ppermute | solution.py:326
  77.0 1.2 %collective-permute-start.22 = (f32[16,256]{1,0:T(8,128)S(1)}, f32[16,256]{1,0:T(8,128)S(1)}, u32[]{:S(2)}, u32[]{:S(2)}) collective-permute-start(f32[16,256]{1,0:T(8,128)S(1)} %add_add_fusion.1.refs_0_), channel_id=1, source_target_pairs={{0,4},{4,0},{8,12},{12,8},{16,20},{20,16},{24,28},{28,24},{1,5},{5... | collective-permute-start | bytes 49160 | tf_op jit(solution)/shard_map/ppermute | solution.py:295
  79.0 5.6 %collective-permute-start.23 = (f32[16,256]{1,0:T(8,128)S(1)}, f32[16,256]{1,0:T(8,128)S(1)}, u32[]{:S(2)}, u32[]{:S(2)}) collective-permute-start(f32[16,256]{1,0:T(8,128)S(1)} %row_2.1.refs_6_), channel_id=1, source_target_pairs={{0,3},{1,2},{2,1},{3,0},{4,5},{5,4},{6,7},{7,6},{8,11},{9,10},{10,... | collective-permute-start | bytes 49160 | tf_op jit(solution)/shard_map/ppermute | solution.py:326
  81.4 4.6 %collective-permute-start.24 = (f32[16,256]{1,0:T(8,128)S(1)}, f32[16,256]{1,0:T(8,128)S(1)}, u32[]{:S(2)}, u32[]{:S(2)}) collective-permute-start(f32[16,256]{1,0:T(8,128)S(1)} %row_2.1.refs_6_), channel_id=1, source_target_pairs={{0,2},{1,3},{2,0},{3,1},{4,7},{5,6},{6,5},{7,4},{8,10},{9,11},{10,... | collective-permute-start | bytes 49160 | tf_op jit(solution)/shard_map/ppermute | solution.py:326
  82.4 3.9 %collective-permute-start.25 = (f32[16,256]{1,0:T(8,128)S(1)}, f32[16,256]{1,0:T(8,128)S(1)}, u32[]{:S(2)}, u32[]{:S(2)}) collective-permute-start(f32[16,256]{1,0:T(8,128)S(1)} %row_2.1.refs_6_), channel_id=1, source_target_pairs={{0,1},{1,0},{2,3},{3,2},{4,6},{5,7},{6,4},{7,5},{8,9},{9,8},{10,11... | collective-permute-start | bytes 49160 | tf_op jit(solution)/shard_map/ppermute | solution.py:326
  87.1 4.7 %collective-permute-start.26 = (f32[16,256]{1,0:T(8,128)S(1)}, f32[16,256]{1,0:T(8,128)S(1)}, u32[]{:S(2)}, u32[]{:S(2)}) collective-permute-start(f32[16,256]{1,0:T(8,128)S(1)} %get-tuple-element.55), channel_id=1, source_target_pairs={{0,24},{1,25},{2,26},{3,27},{4,12},{5,13},{6,14},{7,15},{8,16},{9,... | collective-permute-start | bytes 49160 | tf_op jit(solution)/shard_map/ppermute | solution.py:326
  89.6 3.7 %collective-permute-start.27 = (f32[16,256]{1,0:T(8,128)S(1)}, f32[16,256]{1,0:T(8,128)S(1)}, u32[]{:S(2)}, u32[]{:S(2)}) collective-permute-start(f32[16,256]{1,0:T(8,128)S(1)} %get-tuple-element.55), channel_id=1, source_target_pairs={{0,16},{1,17},{2,18},{3,19},{4,28},{5,29},{6,30},{7,31},{8,24},{9,... | collective-permute-start | bytes 49160 | tf_op jit(solution)/shard_map/ppermute | solution.py:326
  90.0 3.7 %collective-permute-start.28 = (f32[16,256]{1,0:T(8,128)S(1)}, f32[16,256]{1,0:T(8,128)S(1)}, u32[]{:S(2)}, u32[]{:S(2)}) collective-permute-start(f32[16,256]{1,0:T(8,128)S(1)} %get-tuple-element.55), channel_id=1, source_target_pairs={{0,8},{1,9},{2,10},{3,11},{4,20},{5,21},{6,22},{7,23},{8,0},{9,1},... | collective-permute-start | bytes 49160 | tf_op jit(solution)/shard_map/ppermute | solution.py:326
  93.8 1.2 %collective-permute-start.29 = (f32[16,256]{1,0:T(8,128)S(1)}, f32[16,256]{1,0:T(8,128)S(1)}, u32[]{:S(2)}, u32[]{:S(2)}) collective-permute-start(f32[16,256]{1,0:T(8,128)S(1)} %add_add_fusion.refs_0_), channel_id=1, source_target_pairs={{0,4},{4,0},{8,12},{12,8},{16,20},{20,16},{24,28},{28,24},{1,5},{5... | collective-permute-start | bytes 49160 | tf_op jit(solution)/shard_map/ppermute | solution.py:295
  (7 other events, 38.7 us)

commit v4 on v3

--- a/solution.py
+++ b/solution.py
@@ -10,8 +10,8 @@
 
 TILE = 256
 LANES = 128
-STRIP = 32
-FINE = 16
+STRIP = 16
+FINE = 32
 HALF = 64
 LOW = -1e30
 FLOOR = -1e29

time: 95.8 us -> 95.8 us (level)
  no operation moved by 1% of the time
where the time goes in v4:
time: 95.8 us; the launch traced here: 95.6 us
  waiting for transfers between devices  36.8 us (38%)
  starting transfers between devices  33.9 us (35%)
  Pallas kernels  17.1 us (18%)
  local copies, waits for them, and re-layouts  6.63 us (7%)
    ppermute x18, starting transfers between devices, exchange(): parts.append(lax.ppermute(x, ('row', 'col'), pairs))  24.4 us
    ppermute x12, waiting for transfers between devices, permute(): return lax.ppermute(x, axis, [(i, partner(i)) for i in range(n)])  20.5 us
    pallas_call x10, Pallas kernels, kernel_call(): pl.pallas_call(body, out_shape=[(jax.ShapeDtypeStruct if final else VMEM)...  17.1 us
    ppermute x18, waiting for transfers between devices, exchange(): parts.append(lax.ppermute(x, ('row', 'col'), pairs))  16.4 us
    ppermute x12, starting transfers between devices, permute(): return lax.ppermute(x, axis, [(i, partner(i)) for i in range(n)])  9.58 us
    unnamed x19, local copies, waits for them, and re-layouts  6.57 us
  transfers between devices with their start and end apart: 30, of which 23 were waited for; matrix products, arithmetic and copies ran while one was open for 1% of the time, Pallas kernels for 8%

profile of v4, /device:TPU:0, one launch (start us, length us, event | category | flops | bytes accessed | tf_op | source)
XLA Modules:
  0.0 95.6 jit_solution(11270363232464955051)
XLA Ops:
  0.7 3.0 %collective-permute-start = (bf16[4096,128]{1,0:T(8,128)(2,1)}, bf16[4096,128]{1,0:T(8,128)(2,1)S(1)}, u32[]{:S(2)}, u32[]{:S(2)}) collective-permute-start(bf16[4096,128]{1,0:T(8,128)(2,1)} %refs_3_.1), channel_id=1, source_target_pairs={{0,8},{4,20},{8,0},{12,28},{16,24},{20,4},{24,16},{28,12},{1,9},{5... | collective-permute-start | bytes 3145736 | tf_op jit(solution)/shard_map/ppermute | solution.py:295
  3.7 3.4 %copy-done = bf16[4096,1024]{1,0:T(8,128)(2,1)S(1)} copy-done((bf16[4096,1024]{1,0:T(8,128)(2,1)S(1)}, bf16[4096,1024]{1,0:T(8,128)(2,1)}, u32[]{:S(2)}) %copy-start) | copy-done | bytes 8388632
  7.0 1.2 %copy-done.2 = bf16[4096,128]{1,0:T(8,128)(2,1)S(1)} copy-done((bf16[4096,128]{1,0:T(8,128)(2,1)S(1)}, bf16[4096,128]{1,0:T(8,128)(2,1)}, u32[]{:S(2)}) %copy-start.2) | copy-done | bytes 1048600
  9.6 2.4 %score_1_False.1 = (f32[16,2,256,256]{3,2,1,0:T(8,128)S(1)}, f32[32,256]{1,0:T(8,128)S(1)}) custom-call(s32[2,16]{1,0:T(2,128)S(1)} %bitcast.17, s32[1,16]{1,0:T(1,128)S(1)} %bitcast.20, bf16[4096,1024]{1,0:T(8,128)(2,1)S(1)} %copy-done, bf16[4096,128]{1,0:T(8,128)(2,1)S(1)} %copy-done.2), custom_call_target="tpu_custom_call" | custom-call | flops 8192 | bytes 1024 | tf_op jit(solution)/shard_map/score_1_False/pallas_call | solution.py:37
  12.0 1.6 %collective-permute-start.1 = (bf16[4096,128]{1,0:T(8,128)(2,1)S(1)}, bf16[4096,128]{1,0:T(8,128)(2,1)S(1)}, u32[]{:S(2)}, u32[]{:S(2)}) collective-permute-start(bf16[4096,128]{1,0:T(8,128)(2,1)S(1)} %copy-done.2), channel_id=1, source_target_pairs={{0,16},{4,12},{8,24},{12,4},{16,0},{20,28},{24,8},{28,20},{1,17},{... | collective-permute-start | bytes 3145736 | tf_op jit(solution)/shard_map/ppermute | solution.py:295
  13.6 5.6 %collective-permute-done.refs_4_ = bf16[4096,128]{1,0:T(8,128)(2,1)S(1)} collective-permute-done((bf16[4096,128]{1,0:T(8,128)(2,1)}, bf16[4096,128]{1,0:T(8,128)(2,1)S(1)}, u32[]{:S(2)}, u32[]{:S(2)}) %collective-permute-start) | collective-permute-done | bytes 1048608 | tf_op jit(solution)/shard_map/ppermute | solution.py:295
  19.2 1.6 %collective-permute-start.2 = (bf16[2048,128]{1,0:T(8,128)(2,1)S(1)}, bf16[2048,128]{1,0:T(8,128)(2,1)S(1)}, u32[]{:S(2)}, u32[]{:S(2)}) collective-permute-start(bf16[2048,128]{1,0:T(8,128)(2,1)S(1)} %get-tuple-element.57), channel_id=1, source_target_pairs={{0,16},{4,12},{8,24},{12,4},{16,0},{20,28},{24,8},{28,20},{1,17},{... | collective-permute-start | bytes 1572872 | tf_op jit(solution)/shard_map/ppermute | solution.py:295
  20.9 6.2 %collective-permute-done.1.refs_3_ = bf16[4096,128]{1,0:T(8,128)(2,1)S(1)} collective-permute-done((bf16[4096,128]{1,0:T(8,128)(2,1)S(1)}, bf16[4096,128]{1,0:T(8,128)(2,1)S(1)}, u32[]{:S(2)}, u32[]{:S(2)}) %collective-permute-start.1) | collective-permute-done | bytes 1048608 | tf_op jit(solution)/shard_map/ppermute | solution.py:295
  27.1 1.7 %collective-permute-start.6 = (bf16[2048,128]{1,0:T(8,128)(2,1)S(1)}, bf16[2048,128]{1,0:T(8,128)(2,1)S(1)}, u32[]{:S(2)}, u32[]{:S(2)}) collective-permute-start(bf16[2048,128]{1,0:T(8,128)(2,1)S(1)} %get-tuple-element.56), channel_id=1, source_target_pairs={{0,16},{4,12},{8,24},{12,4},{16,0},{20,28},{24,8},{28,20},{1,17},{... | collective-permute-start | bytes 1572872 | tf_op jit(solution)/shard_map/ppermute | solution.py:295
  28.8 4.3 %score_3_False.1 = (f32[16,2,256,256]{3,2,1,0:T(8,128)S(1)}, f32[8,128]{1,0:T(8,128)}) custom-call(s32[2,16]{1,0:T(2,128)S(1)} %bitcast.18, s32[1,16]{1,0:T(1,128)S(1)} %bitcast.21, bf16[4096,1024]{1,0:T(8,128)(2,1)S(1)} %copy-done.1, bf16[4096,128]{1,0:T(8,128)(2,1)S(1)} %collective-permute-done.3.refs_3_, ...), custom_call_target="tpu_custom_call" | custom-call | flops 8192 | bytes 1024 | tf_op jit(solution)/shard_map/score_3_False/pallas_call | solution.py:37
  34.0 4.3 %collective-permute-done.6 = bf16[2048,128]{1,0:T(8,128)(2,1)S(1)} collective-permute-done((bf16[2048,128]{1,0:T(8,128)(2,1)S(1)}, bf16[2048,128]{1,0:T(8,128)(2,1)S(1)}, u32[]{:S(2)}, u32[]{:S(2)}) %collective-permute-start.6) | collective-permute-done | bytes 524320 | tf_op jit(solution)/shard_map/ppermute | solution.py:295
  39.0 1.5 %collective-permute-done.8 = bf16[2048,128]{1,0:T(8,128)(2,1)S(1)} collective-permute-done((bf16[2048,128]{1,0:T(8,128)(2,1)S(1)}, bf16[2048,128]{1,0:T(8,128)(2,1)S(1)}, u32[]{:S(2)}, u32[]{:S(2)}) %collective-permute-start.8) | collective-permute-done | bytes 524320 | tf_op jit(solution)/shard_map/ppermute | solution.py:295
  40.6 4.2 %score_4_True.1 = (f32[16,2,256,256]{3,2,1,0:T(8,128)S(1)}, f32[2,16,256]{2,1,0:T(8,128)S(1)}) custom-call(s32[2,16]{1,0:T(2,128)S(1)} %bitcast.19, s32[1,16]{1,0:T(1,128)S(1)} %bitcast.22, bf16[4096,1024]{1,0:T(8,128)(2,1)S(1)} %copy-done.1, bf16[4096,128]{1,0:T(8,128)(2,1)S(1)} %collective-permute-done.1.refs_3_, ...), custom_call_target="tpu_custom_call" | custom-call | flops 8192 | bytes 1024 | tf_op jit(solution)/shard_map/score_4_True/pallas_call | solution.py:37
  44.7 4.2 %collective-permute-start.10 = (f32[2,16,256]{2,1,0:T(8,128)S(1)}, f32[2,16,256]{2,1,0:T(8,128)S(1)}, u32[]{:S(2)}, u32[]{:S(2)}) collective-permute-start(f32[2,16,256]{2,1,0:T(8,128)S(1)} %get-tuple-element.45.stats.refs_0_), channel_id=1, source_target_pairs={{0,3},{1,2},{2,1},{3,0},{4,5},{5,4},{6,7},{7,6},{8,11},{9,10},{10,... | collective-permute-start | bytes 98312 | tf_op jit(solution)/shard_map/ppermute | solution.py:326
  49.6 1.2 %exps.1.before = f32[16,2,256,256]{3,2,1,0:T(8,128)S(1)} custom-call(f32[16,2,256,256]{3,2,1,0:T(8,128)S(1)} %get-tuple-element.44.score, f32[2,16,256]{2,1,0:T(8,128)S(1)} %get-tuple-element.45.stats.refs_0_), custom_call_target="tpu_custom_call" | custom-call | flops 8192 | bytes 1024 | tf_op jit(solution)/shard_map/exps/pallas_call | solution.py:37
  51.1 2.6 %collective-permute-done.11.refs_3_ = f32[2,16,256]{2,1,0:T(8,128)S(1)} collective-permute-done((f32[2,16,256]{2,1,0:T(8,128)S(1)}, f32[2,16,256]{2,1,0:T(8,128)S(1)}, u32[]{:S(2)}, u32[]{:S(2)}) %collective-permute-start.11) | collective-permute-done | bytes 32800 | tf_op jit(solution)/shard_map/ppermute | solution.py:326
  53.8 1.2 %column_0.1 = (f32[16,2,256,256]{3,2,1,0:T(8,128)S(1)}, f32[2,16,256]{2,1,0:T(8,128)S(1)}, f32[32,256]{1,0:T(8,128)S(1)}, f32[16,256]{1,0:T(8,128)S(1)}, f32[16,256]{1,0:T(8,128)S(1)}) custom-call(f32[32,256]{1,0:T(8,128)S(1)} %get-tuple-element.32.names.refs_0_, f32[16,2,256,256]{3,2,1,0:T(8,128)S(1)} %get-tuple-element.44.score, ...), custom_call_target="tpu_custom_call", output_to_operand_aliasing={{0}: (2, {})} | custom-call | flops 8192 | bytes 1024 | tf_op jit(solution)/shard_map/column_0/pallas_call | solution.py:37
  55.0 2.5 %collective-permute-start.12 = (f32[2,16,256]{2,1,0:T(8,128)S(1)}, f32[2,16,256]{2,1,0:T(8,128)S(1)}, u32[]{:S(2)}, u32[]{:S(2)}) collective-permute-start(f32[2,16,256]{2,1,0:T(8,128)S(1)} %get-tuple-element.49), channel_id=1, source_target_pairs={{0,24},{1,25},{2,26},{3,27},{4,12},{5,13},{6,14},{7,15},{8,16},{9,... | collective-permute-start | bytes 98312 | tf_op jit(solution)/shard_map/ppermute | solution.py:326
  58.6 1.6 %collective-permute-done.12 = f32[2,16,256]{2,1,0:T(8,128)S(1)} collective-permute-done((f32[2,16,256]{2,1,0:T(8,128)S(1)}, f32[2,16,256]{2,1,0:T(8,128)S(1)}, u32[]{:S(2)}, u32[]{:S(2)}) %collective-permute-start.12) | collective-permute-done | bytes 32800 | tf_op jit(solution)/shard_map/ppermute | solution.py:326
  60.2 1.2 %collective-permute-done.13 = f32[2,16,256]{2,1,0:T(8,128)S(1)} collective-permute-done((f32[2,16,256]{2,1,0:T(8,128)S(1)}, f32[2,16,256]{2,1,0:T(8,128)S(1)}, u32[]{:S(2)}, u32[]{:S(2)}) %collective-permute-start.13) | collective-permute-done | bytes 32800 | tf_op jit(solution)/shard_map/ppermute | solution.py:326
  61.9 1.2 %collective-permute-done.15.refs_1_ = f32[2,16,256]{2,1,0:T(8,128)S(1)} collective-permute-done((f32[2,16,256]{2,1,0:T(8,128)S(1)}, f32[2,16,256]{2,1,0:T(8,128)S(1)}, u32[]{:S(2)}, u32[]{:S(2)}) %collective-permute-start.15) | collective-permute-done | bytes 32800 | tf_op jit(solution)/shard_map/ppermute | solution.py:295
  63.9 1.6 %collective-permute-start.16 = (f32[16,256]{1,0:T(8,128)S(1)}, f32[16,256]{1,0:T(8,128)S(1)}, u32[]{:S(2)}, u32[]{:S(2)}) collective-permute-start(f32[16,256]{1,0:T(8,128)S(1)} %get-tuple-element.52.refs_5_), channel_id=1, source_target_pairs={{0,3},{1,2},{2,1},{3,0},{4,5},{5,4},{6,7},{7,6},{8,11},{9,10},{10,... | collective-permute-start | bytes 49160 | tf_op jit(solution)/shard_map/ppermute | solution.py:326
  66.0 2.3 %collective-permute-start.18 = (f32[16,256]{1,0:T(8,128)S(1)}, f32[16,256]{1,0:T(8,128)S(1)}, u32[]{:S(2)}, u32[]{:S(2)}) collective-permute-start(f32[16,256]{1,0:T(8,128)S(1)} %get-tuple-element.52.refs_5_), channel_id=1, source_target_pairs={{0,1},{1,0},{2,3},{3,2},{4,6},{5,7},{6,4},{7,5},{8,9},{9,8},{10,11... | collective-permute-start | bytes 49160 | tf_op jit(solution)/shard_map/ppermute | solution.py:326
  68.3 1.3 %collective-permute-done.16.refs_6_ = f32[16,256]{1,0:T(8,128)S(1)} collective-permute-done((f32[16,256]{1,0:T(8,128)S(1)}, f32[16,256]{1,0:T(8,128)S(1)}, u32[]{:S(2)}, u32[]{:S(2)}) %collective-permute-start.16) | collective-permute-done | bytes 16416 | tf_op jit(solution)/shard_map/ppermute | solution.py:326
  71.1 1.6 %collective-permute-start.19 = (f32[16,256]{1,0:T(8,128)S(1)}, f32[16,256]{1,0:T(8,128)S(1)}, u32[]{:S(2)}, u32[]{:S(2)}) collective-permute-start(f32[16,256]{1,0:T(8,128)S(1)} %column_1.1), channel_id=1, source_target_pairs={{0,24},{1,25},{2,26},{3,27},{4,12},{5,13},{6,14},{7,15},{8,16},{9,... | collective-permute-start | bytes 49160 | tf_op jit(solution)/shard_map/ppermute | solution.py:326
  73.3 1.4 %collective-permute-start.21 = (f32[16,256]{1,0:T(8,128)S(1)}, f32[16,256]{1,0:T(8,128)S(1)}, u32[]{:S(2)}, u32[]{:S(2)}) collective-permute-start(f32[16,256]{1,0:T(8,128)S(1)} %column_1.1), channel_id=1, source_target_pairs={{0,8},{1,9},{2,10},{3,11},{4,20},{5,21},{6,22},{7,23},{8,0},{9,1},... | collective-permute-start | bytes 49160 | tf_op jit(solution)/shard_map/ppermute | solution.py:326
  77.1 1.2 %collective-permute-done.22.refs_1_ = f32[16,256]{1,0:T(8,128)S(1)} collective-permute-done((f32[16,256]{1,0:T(8,128)S(1)}, f32[16,256]{1,0:T(8,128)S(1)}, u32[]{:S(2)}, u32[]{:S(2)}) %collective-permute-start.22) | collective-permute-done | bytes 16416 | tf_op jit(solution)/shard_map/ppermute | solution.py:295
  79.0 2.4 %collective-permute-start.23 = (f32[16,256]{1,0:T(8,128)S(1)}, f32[16,256]{1,0:T(8,128)S(1)}, u32[]{:S(2)}, u32[]{:S(2)}) collective-permute-start(f32[16,256]{1,0:T(8,128)S(1)} %row_2.1.refs_6_), channel_id=1, source_target_pairs={{0,3},{1,2},{2,1},{3,0},{4,5},{5,4},{6,7},{7,6},{8,11},{9,10},{10,... | collective-permute-start | bytes 49160 | tf_op jit(solution)/shard_map/ppermute | solution.py:326
  84.6 1.5 %collective-permute-done.24.refs_8_ = f32[16,256]{1,0:T(8,128)S(1)} collective-permute-done((f32[16,256]{1,0:T(8,128)S(1)}, f32[16,256]{1,0:T(8,128)S(1)}, u32[]{:S(2)}, u32[]{:S(2)}) %collective-permute-start.24) | collective-permute-done | bytes 16416 | tf_op jit(solution)/shard_map/ppermute | solution.py:326
  87.1 2.5 %collective-permute-start.26 = (f32[16,256]{1,0:T(8,128)S(1)}, f32[16,256]{1,0:T(8,128)S(1)}, u32[]{:S(2)}, u32[]{:S(2)}) collective-permute-start(f32[16,256]{1,0:T(8,128)S(1)} %get-tuple-element.55), channel_id=1, source_target_pairs={{0,24},{1,25},{2,26},{3,27},{4,12},{5,13},{6,14},{7,15},{8,16},{9,... | collective-permute-start | bytes 49160 | tf_op jit(solution)/shard_map/ppermute | solution.py:326
  90.7 1.3 %collective-permute-done.26 = f32[16,256]{1,0:T(8,128)S(1)} collective-permute-done((f32[16,256]{1,0:T(8,128)S(1)}, f32[16,256]{1,0:T(8,128)S(1)}, u32[]{:S(2)}, u32[]{:S(2)}) %collective-permute-start.26) | collective-permute-done | bytes 16416 | tf_op jit(solution)/shard_map/ppermute | solution.py:326
  91.9 1.4 %collective-permute-done.27 = f32[16,256]{1,0:T(8,128)S(1)} collective-permute-done((f32[16,256]{1,0:T(8,128)S(1)}, f32[16,256]{1,0:T(8,128)S(1)}, u32[]{:S(2)}, u32[]{:S(2)}) %collective-permute-start.27) | collective-permute-done | bytes 16416 | tf_op jit(solution)/shard_map/ppermute | solution.py:326
  (65 shorter events, 19.8 us)
Async XLA Ops:
  0.6 28.2 %copy-start.6 = (s32[16,2]{0,1:T(2,128)S(1)}, s32[16,2]{0,1:T(2,128)}, u32[]{:S(2)}) copy-start(s32[16,2]{0,1:T(2,128)} %param.10) | copy-start | bytes 388
  0.6 28.2 %copy-start.8 = (s32[16,1]{0,1:T(1,128)S(1)}, s32[16,1]{0,1:T(1,128)}, u32[]{:S(2)}) copy-start(s32[16,1]{0,1:T(1,128)} %param.11) | copy-start | bytes 196
  0.7 18.5 %collective-permute-start = (bf16[4096,128]{1,0:T(8,128)(2,1)}, bf16[4096,128]{1,0:T(8,128)(2,1)S(1)}, u32[]{:S(2)}, u32[]{:S(2)}) collective-permute-start(bf16[4096,128]{1,0:T(8,128)(2,1)} %refs_3_.1), channel_id=1, source_target_pairs={{0,8},{4,20},{8,0},{12,28},{16,24},{20,4},{24,16},{28,12},{1,9},{5... | collective-permute-start | bytes 3145736 | tf_op jit(solution)/shard_map/ppermute | solution.py:295
  3.7 25.1 %collective-permute-start.3 = (bf16[4096,128]{1,0:T(8,128)(2,1)}, bf16[4096,128]{1,0:T(8,128)(2,1)S(1)}, u32[]{:S(2)}, u32[]{:S(2)}) collective-permute-start(bf16[4096,128]{1,0:T(8,128)(2,1)} %refs_3_.1), channel_id=1, source_target_pairs={{0,4},{4,0},{8,12},{12,8},{16,20},{20,16},{24,28},{28,24},{1,5},{5... | collective-permute-start | bytes 3145736 | tf_op jit(solution)/shard_map/ppermute | solution.py:295
  12.0 15.1 %collective-permute-start.1 = (bf16[4096,128]{1,0:T(8,128)(2,1)S(1)}, bf16[4096,128]{1,0:T(8,128)(2,1)S(1)}, u32[]{:S(2)}, u32[]{:S(2)}) collective-permute-start(bf16[4096,128]{1,0:T(8,128)(2,1)S(1)} %copy-done.2), channel_id=1, source_target_pairs={{0,16},{4,12},{8,24},{12,4},{16,0},{20,28},{24,8},{28,20},{1,17},{... | collective-permute-start | bytes 3145736 | tf_op jit(solution)/shard_map/ppermute | solution.py:295
  19.2 9.6 %collective-permute-start.4 = (bf16[4096,128]{1,0:T(8,128)(2,1)S(1)}, bf16[4096,128]{1,0:T(8,128)(2,1)S(1)}, u32[]{:S(2)}, u32[]{:S(2)}) collective-permute-start(bf16[4096,128]{1,0:T(8,128)(2,1)S(1)} %collective-permute-done.refs_4_), channel_id=1, source_target_pairs={{0,4},{4,0},{8,12},{12,8},{16,20},{20,16},{24,28},{28,24},{1,5},{5... | collective-permute-start | bytes 3145736 | tf_op jit(solution)/shard_map/ppermute | solution.py:295
  19.2 13.8 %collective-permute-start.2 = (bf16[2048,128]{1,0:T(8,128)(2,1)S(1)}, bf16[2048,128]{1,0:T(8,128)(2,1)S(1)}, u32[]{:S(2)}, u32[]{:S(2)}) collective-permute-start(bf16[2048,128]{1,0:T(8,128)(2,1)S(1)} %get-tuple-element.57), channel_id=1, source_target_pairs={{0,16},{4,12},{8,24},{12,4},{16,0},{20,28},{24,8},{28,20},{1,17},{... | collective-permute-start | bytes 1572872 | tf_op jit(solution)/shard_map/ppermute | solution.py:295
  27.1 11.2 %collective-permute-start.6 = (bf16[2048,128]{1,0:T(8,128)(2,1)S(1)}, bf16[2048,128]{1,0:T(8,128)(2,1)S(1)}, u32[]{:S(2)}, u32[]{:S(2)}) collective-permute-start(bf16[2048,128]{1,0:T(8,128)(2,1)S(1)} %get-tuple-element.56), channel_id=1, source_target_pairs={{0,16},{4,12},{8,24},{12,4},{16,0},{20,28},{24,8},{28,20},{1,17},{... | collective-permute-start | bytes 1572872 | tf_op jit(solution)/shard_map/ppermute | solution.py:295
  33.1 5.2 %collective-permute-start.7 = (bf16[2048,128]{1,0:T(8,128)(2,1)S(1)}, bf16[2048,128]{1,0:T(8,128)(2,1)S(1)}, u32[]{:S(2)}, u32[]{:S(2)}) collective-permute-start(bf16[2048,128]{1,0:T(8,128)(2,1)S(1)} %collective-permute-done.2), channel_id=1, source_target_pairs={{0,4},{4,0},{8,12},{12,8},{16,20},{20,16},{24,28},{28,24},{1,5},{5... | collective-permute-start | bytes 1572872 | tf_op jit(solution)/shard_map/ppermute | solution.py:295
  34.0 6.5 %collective-permute-start.5 = (bf16[4096,128]{1,0:T(8,128)(2,1)S(1)}, bf16[4096,128]{1,0:T(8,128)(2,1)S(1)}, u32[]{:S(2)}, u32[]{:S(2)}) collective-permute-start(bf16[4096,128]{1,0:T(8,128)(2,1)S(1)} %collective-permute-done.1.refs_3_), channel_id=1, source_target_pairs={{0,4},{4,0},{8,12},{12,8},{16,20},{20,16},{24,28},{28,24},{1,5},{5... | collective-permute-start | bytes 3145736 | tf_op jit(solution)/shard_map/ppermute | solution.py:295
  38.3 2.2 %collective-permute-start.8 = (bf16[2048,128]{1,0:T(8,128)(2,1)S(1)}, bf16[2048,128]{1,0:T(8,128)(2,1)S(1)}, u32[]{:S(2)}, u32[]{:S(2)}) collective-permute-start(bf16[2048,128]{1,0:T(8,128)(2,1)S(1)} %collective-permute-done.6), channel_id=1, source_target_pairs={{0,4},{4,0},{8,12},{12,8},{16,20},{20,16},{24,28},{28,24},{1,5},{5... | collective-permute-start | bytes 1572872 | tf_op jit(solution)/shard_map/ppermute | solution.py:295
  44.7 6.4 %collective-permute-start.10 = (f32[2,16,256]{2,1,0:T(8,128)S(1)}, f32[2,16,256]{2,1,0:T(8,128)S(1)}, u32[]{:S(2)}, u32[]{:S(2)}) collective-permute-start(f32[2,16,256]{2,1,0:T(8,128)S(1)} %get-tuple-element.45.stats.refs_0_), channel_id=1, source_target_pairs={{0,3},{1,2},{2,1},{3,0},{4,5},{5,4},{6,7},{7,6},{8,11},{9,10},{10,... | collective-permute-start | bytes 98312 | tf_op jit(solution)/shard_map/ppermute | solution.py:326
  48.9 4.8 %collective-permute-start.11 = (f32[2,16,256]{2,1,0:T(8,128)S(1)}, f32[2,16,256]{2,1,0:T(8,128)S(1)}, u32[]{:S(2)}, u32[]{:S(2)}) collective-permute-start(f32[2,16,256]{2,1,0:T(8,128)S(1)} %get-tuple-element.45.stats.refs_0_), channel_id=1, source_target_pairs={{0,2},{1,3},{2,0},{3,1},{4,7},{5,6},{6,5},{7,4},{8,10},{9,11},{10,... | collective-permute-start | bytes 98312 | tf_op jit(solution)/shard_map/ppermute | solution.py:326
  48.9 4.8 %collective-permute-start.9 = (f32[2,16,256]{2,1,0:T(8,128)S(1)}, f32[2,16,256]{2,1,0:T(8,128)S(1)}, u32[]{:S(2)}, u32[]{:S(2)}) collective-permute-start(f32[2,16,256]{2,1,0:T(8,128)S(1)} %get-tuple-element.45.stats.refs_0_), channel_id=1, source_target_pairs={{0,1},{1,0},{2,3},{3,2},{4,6},{5,7},{6,4},{7,5},{8,9},{9,8},{10,11... | collective-permute-start | bytes 98312 | tf_op jit(solution)/shard_map/ppermute | solution.py:326
  55.0 5.2 %collective-permute-start.12 = (f32[2,16,256]{2,1,0:T(8,128)S(1)}, f32[2,16,256]{2,1,0:T(8,128)S(1)}, u32[]{:S(2)}, u32[]{:S(2)}) collective-permute-start(f32[2,16,256]{2,1,0:T(8,128)S(1)} %get-tuple-element.49), channel_id=1, source_target_pairs={{0,24},{1,25},{2,26},{3,27},{4,12},{5,13},{6,14},{7,15},{8,16},{9,... | collective-permute-start | bytes 98312 | tf_op jit(solution)/shard_map/ppermute | solution.py:326
  57.5 3.9 %collective-permute-start.13 = (f32[2,16,256]{2,1,0:T(8,128)S(1)}, f32[2,16,256]{2,1,0:T(8,128)S(1)}, u32[]{:S(2)}, u32[]{:S(2)}) collective-permute-start(f32[2,16,256]{2,1,0:T(8,128)S(1)} %get-tuple-element.49), channel_id=1, source_target_pairs={{0,16},{1,17},{2,18},{3,19},{4,28},{5,29},{6,30},{7,31},{8,24},{9,... | collective-permute-start | bytes 98312 | tf_op jit(solution)/shard_map/ppermute | solution.py:326
  57.9 3.9 %collective-permute-start.14 = (f32[2,16,256]{2,1,0:T(8,128)S(1)}, f32[2,16,256]{2,1,0:T(8,128)S(1)}, u32[]{:S(2)}, u32[]{:S(2)}) collective-permute-start(f32[2,16,256]{2,1,0:T(8,128)S(1)} %get-tuple-element.49), channel_id=1, source_target_pairs={{0,8},{1,9},{2,10},{3,11},{4,20},{5,21},{6,22},{7,23},{8,0},{9,1},... | collective-permute-start | bytes 98312 | tf_op jit(solution)/shard_map/ppermute | solution.py:326
  61.9 1.2 %collective-permute-start.15 = (f32[2,16,256]{2,1,0:T(8,128)S(1)}, f32[2,16,256]{2,1,0:T(8,128)S(1)}, u32[]{:S(2)}, u32[]{:S(2)}) collective-permute-start(f32[2,16,256]{2,1,0:T(8,128)S(1)} %broadcast_select_fusion.refs_0_), channel_id=1, source_target_pairs={{0,4},{4,0},{8,12},{12,8},{16,20},{20,16},{24,28},{28,24},{1,5},{5... | collective-permute-start | bytes 98312 | tf_op jit(solution)/shard_map/ppermute | solution.py:295
  63.9 5.7 %collective-permute-start.16 = (f32[16,256]{1,0:T(8,128)S(1)}, f32[16,256]{1,0:T(8,128)S(1)}, u32[]{:S(2)}, u32[]{:S(2)}) collective-permute-start(f32[16,256]{1,0:T(8,128)S(1)} %get-tuple-element.52.refs_5_), channel_id=1, source_target_pairs={{0,3},{1,2},{2,1},{3,0},{4,5},{5,4},{6,7},{7,6},{8,11},{9,10},{10,... | collective-permute-start | bytes 49160 | tf_op jit(solution)/shard_map/ppermute | solution.py:326
  65.6 4.7 %collective-permute-start.17 = (f32[16,256]{1,0:T(8,128)S(1)}, f32[16,256]{1,0:T(8,128)S(1)}, u32[]{:S(2)}, u32[]{:S(2)}) collective-permute-start(f32[16,256]{1,0:T(8,128)S(1)} %get-tuple-element.52.refs_5_), channel_id=1, source_target_pairs={{0,2},{1,3},{2,0},{3,1},{4,7},{5,6},{6,5},{7,4},{8,10},{9,11},{10,... | collective-permute-start | bytes 49160 | tf_op jit(solution)/shard_map/ppermute | solution.py:326
  66.0 4.2 %collective-permute-start.18 = (f32[16,256]{1,0:T(8,128)S(1)}, f32[16,256]{1,0:T(8,128)S(1)}, u32[]{:S(2)}, u32[]{:S(2)}) collective-permute-start(f32[16,256]{1,0:T(8,128)S(1)} %get-tuple-element.52.refs_5_), channel_id=1, source_target_pairs={{0,1},{1,0},{2,3},{3,2},{4,6},{5,7},{6,4},{7,5},{8,9},{9,8},{10,11... | collective-permute-start | bytes 49160 | tf_op jit(solution)/shard_map/ppermute | solution.py:326
  71.1 4.7 %collective-permute-start.19 = (f32[16,256]{1,0:T(8,128)S(1)}, f32[16,256]{1,0:T(8,128)S(1)}, u32[]{:S(2)}, u32[]{:S(2)}) collective-permute-start(f32[16,256]{1,0:T(8,128)S(1)} %column_1.1), channel_id=1, source_target_pairs={{0,24},{1,25},{2,26},{3,27},{4,12},{5,13},{6,14},{7,15},{8,16},{9,... | collective-permute-start | bytes 49160 | tf_op jit(solution)/shard_map/ppermute | solution.py:326
  72.7 3.7 %collective-permute-start.20 = (f32[16,256]{1,0:T(8,128)S(1)}, f32[16,256]{1,0:T(8,128)S(1)}, u32[]{:S(2)}, u32[]{:S(2)}) collective-permute-start(f32[16,256]{1,0:T(8,128)S(1)} %column_1.1), channel_id=1, source_target_pairs={{0,16},{1,17},{2,18},{3,19},{4,28},{5,29},{6,30},{7,31},{8,24},{9,... | collective-permute-start | bytes 49160 | tf_op jit(solution)/shard_map/ppermute | solution.py:326
  73.3 3.7 %collective-permute-start.21 = (f32[16,256]{1,0:T(8,128)S(1)}, f32[16,256]{1,0:T(8,128)S(1)}, u32[]{:S(2)}, u32[]{:S(2)}) collective-permute-start(f32[16,256]{1,0:T(8,128)S(1)} %column_1.1), channel_id=1, source_target_pairs={{0,8},{1,9},{2,10},{3,11},{4,20},{5,21},{6,22},{7,23},{8,0},{9,1},... | collective-permute-start | bytes 49160 | tf_op jit(solution)/shard_map/ppermute | solution.py:326
  77.0 1.2 %collective-permute-start.22 = (f32[16,256]{1,0:T(8,128)S(1)}, f32[16,256]{1,0:T(8,128)S(1)}, u32[]{:S(2)}, u32[]{:S(2)}) collective-permute-start(f32[16,256]{1,0:T(8,128)S(1)} %add_add_fusion.1.refs_0_), channel_id=1, source_target_pairs={{0,4},{4,0},{8,12},{12,8},{16,20},{20,16},{24,28},{28,24},{1,5},{5... | collective-permute-start | bytes 49160 | tf_op jit(solution)/shard_map/ppermute | solution.py:295
  79.0 5.6 %collective-permute-start.23 = (f32[16,256]{1,0:T(8,128)S(1)}, f32[16,256]{1,0:T(8,128)S(1)}, u32[]{:S(2)}, u32[]{:S(2)}) collective-permute-start(f32[16,256]{1,0:T(8,128)S(1)} %row_2.1.refs_6_), channel_id=1, source_target_pairs={{0,3},{1,2},{2,1},{3,0},{4,5},{5,4},{6,7},{7,6},{8,11},{9,10},{10,... | collective-permute-start | bytes 49160 | tf_op jit(solution)/shard_map/ppermute | solution.py:326
  81.4 4.6 %collective-permute-start.24 = (f32[16,256]{1,0:T(8,128)S(1)}, f32[16,256]{1,0:T(8,128)S(1)}, u32[]{:S(2)}, u32[]{:S(2)}) collective-permute-start(f32[16,256]{1,0:T(8,128)S(1)} %row_2.1.refs_6_), channel_id=1, source_target_pairs={{0,2},{1,3},{2,0},{3,1},{4,7},{5,6},{6,5},{7,4},{8,10},{9,11},{10,... | collective-permute-start | bytes 49160 | tf_op jit(solution)/shard_map/ppermute | solution.py:326
  82.4 3.9 %collective-permute-start.25 = (f32[16,256]{1,0:T(8,128)S(1)}, f32[16,256]{1,0:T(8,128)S(1)}, u32[]{:S(2)}, u32[]{:S(2)}) collective-permute-start(f32[16,256]{1,0:T(8,128)S(1)} %row_2.1.refs_6_), channel_id=1, source_target_pairs={{0,1},{1,0},{2,3},{3,2},{4,6},{5,7},{6,4},{7,5},{8,9},{9,8},{10,11... | collective-permute-start | bytes 49160 | tf_op jit(solution)/shard_map/ppermute | solution.py:326
  87.1 4.8 %collective-permute-start.26 = (f32[16,256]{1,0:T(8,128)S(1)}, f32[16,256]{1,0:T(8,128)S(1)}, u32[]{:S(2)}, u32[]{:S(2)}) collective-permute-start(f32[16,256]{1,0:T(8,128)S(1)} %get-tuple-element.55), channel_id=1, source_target_pairs={{0,24},{1,25},{2,26},{3,27},{4,12},{5,13},{6,14},{7,15},{8,16},{9,... | collective-permute-start | bytes 49160 | tf_op jit(solution)/shard_map/ppermute | solution.py:326
  89.6 3.7 %collective-permute-start.27 = (f32[16,256]{1,0:T(8,128)S(1)}, f32[16,256]{1,0:T(8,128)S(1)}, u32[]{:S(2)}, u32[]{:S(2)}) collective-permute-start(f32[16,256]{1,0:T(8,128)S(1)} %get-tuple-element.55), channel_id=1, source_target_pairs={{0,16},{1,17},{2,18},{3,19},{4,28},{5,29},{6,30},{7,31},{8,24},{9,... | collective-permute-start | bytes 49160 | tf_op jit(solution)/shard_map/ppermute | solution.py:326
  90.0 3.7 %collective-permute-start.28 = (f32[16,256]{1,0:T(8,128)S(1)}, f32[16,256]{1,0:T(8,128)S(1)}, u32[]{:S(2)}, u32[]{:S(2)}) collective-permute-start(f32[16,256]{1,0:T(8,128)S(1)} %get-tuple-element.55), channel_id=1, source_target_pairs={{0,8},{1,9},{2,10},{3,11},{4,20},{5,21},{6,22},{7,23},{8,0},{9,1},... | collective-permute-start | bytes 49160 | tf_op jit(solution)/shard_map/ppermute | solution.py:326
  93.8 1.2 %collective-permute-start.29 = (f32[16,256]{1,0:T(8,128)S(1)}, f32[16,256]{1,0:T(8,128)S(1)}, u32[]{:S(2)}, u32[]{:S(2)}) collective-permute-start(f32[16,256]{1,0:T(8,128)S(1)} %add_add_fusion.refs_0_), channel_id=1, source_target_pairs={{0,4},{4,0},{8,12},{12,8},{16,20},{20,16},{24,28},{28,24},{1,5},{5... | collective-permute-start | bytes 49160 | tf_op jit(solution)/shard_map/ppermute | solution.py:295
  (7 other events, 38.7 us)
